TPU v7x, 512 devices: a whole 4x8x8 slice. The times are simulated.
512 devices in a mesh: tiles: 256 (over x, z, y_hi, core), dp: 2 (over y_lo).
Axes of the slice: x: 4, y: 8 (y_hi: 4, y_lo: 2; y = y_hi * 2 + y_lo), z: 8, core: 2. Of those that a mesh axis runs over, the one named last changes fastest.
Arguments:
- fields: bfloat16 [2, 768, 16, 16, 256], P('dp', 'tiles'), may hold values from -6 to 6
- grad_out: bfloat16 [2, 768, 16, 16, 256], P('dp', 'tiles'), may hold values from -6 to 6
- block_count: int32 [256], P('tiles'), may hold values from 1 to 3, as said below
- ocean: int32 [768], P('tiles'), may hold values from 0 to 1, as said below
- kernel: bfloat16 [7, 7, 256], replicated, may hold values from -0.875 to 0.875
- ln_gain: float32 [256], replicated, may hold values from 0.1 to 1.9
- w_in: bfloat16 [256, 1024], replicated, may hold values from -0.375 to 0.375
- w_out: bfloat16 [1024, 256], replicated, may hold values from -0.1875 to 0.1875
- layer_scale: float32 [256], replicated, may hold values from 0.3 to 1.5
Outputs:
- state_next: bfloat16 [2, 768, 16, 16, 256], P('dp', 'tiles')
- grad_fields: bfloat16 [2, 768, 16, 16, 256], P('dp', 'tiles')
- grad_kernel: float32 [7, 7, 256], replicated
- grad_gain: float32 [256], replicated
- grad_w_in: float32 [256, 1024], replicated
- grad_w_out: float32 [1024, 256], replicated
- grad_scale: float32 [256], replicated
Inputs may be any that keep to these rules, and one draw needn't show every extreme that they name: Index i of tiles owns block_count[i] consecutive cycle tiles in its first slots, in the cycle order of the first step; index i and index i + H (i < H, H half the number of entries) own equally many; some index owns 3 and some index owns one. 1 marks an ocean tile; the first and the last cycle tile that each index of tiles owns are ocean.
All inputs are finite; a program needn't handle non-finite values.
Results may differ from a plain program's by a relative error of at most 0.0066.
Values may be sent and summed in bfloat16 or wider, within the bound.
A program may use at most 64 MiB of HBM per device.

v0:
```python
import jax
import jax.numpy as jnp
from jax import lax
from jax.sharding import PartitionSpec as P

HID = 1024
KSIZE = 7


EPS = 1e-06


def passed_along(block, axis, distance):
    devices = range(lax.axis_size(axis))
    route = [(i - distance, i) for i in devices if i - distance in devices]
    return lax.ppermute(block, axis, route)


def from_partner(block, axis, distance):
    count = lax.axis_size(axis)
    route = []
    for low in range(count):
        high = low | 1 << distance
        if high != low and high < count:
            route += [(low, high), (high, low)]
    return lax.ppermute(block, axis, route)


def gelu_tanh(inputs):
    return jax.nn.gelu(inputs, approximate=True)


def depthwise(padded, kernel_f, tile_rows, tile_cols):
    running = jnp.zeros(padded.shape[:-3] + (tile_rows, tile_cols, padded.shape[-1]), jnp.float32)
    for row_shift in range(KSIZE):
        for col_shift in range(KSIZE):
            window = padded[
                ..., row_shift : row_shift + tile_rows, col_shift : col_shift + tile_cols, :
            ]
            running = running + kernel_f[row_shift, col_shift] * window.astype(jnp.float32)
    return running


def kernel_terms(conv_grad, padded, tile_rows, tile_cols):
    grad_f = conv_grad.astype(jnp.float32)
    leading = tuple(range(grad_f.ndim - 1))
    stacked = []
    for row_shift in range(KSIZE):
        taps = []
        for col_shift in range(KSIZE):
            window = padded[
                ..., row_shift : row_shift + tile_rows, col_shift : col_shift + tile_cols, :
            ]
            taps.append(jnp.sum(grad_f * window.astype(jnp.float32), axis=leading))
        stacked.append(jnp.stack(taps))
    return jnp.stack(stacked)


def spread(conv_grad, kernel_f, tile_rows, tile_cols):
    reach = KSIZE - 1
    widths = [(0, 0)] * (conv_grad.ndim - 3) + [(reach, reach), (reach, reach), (0, 0)]
    grad_f = jnp.pad(conv_grad.astype(jnp.float32), widths)
    running = jnp.zeros(
        conv_grad.shape[:-3] + (tile_rows + reach, tile_cols + reach, conv_grad.shape[-1]),
        jnp.float32,
    )
    for row_shift in range(KSIZE):
        for col_shift in range(KSIZE):
            window = grad_f[
                ...,
                reach - row_shift : reach - row_shift + tile_rows + reach,
                reach - col_shift : reach - col_shift + tile_cols + reach,
                :,
            ]
            running = running + kernel_f[row_shift, col_shift] * window
    return running


def make_block(ln_gain, w_in, w_out, layer_scale):

    def block_step(totals, inputs):
        convolved, skip_rows, cell_mask, tangent = inputs
        row_mean = jnp.mean(convolved, axis=-1, keepdims=True)
        centred = convolved - row_mean
        variance = jnp.mean(centred * centred, axis=-1, keepdims=True)
        inverse = lax.rsqrt(variance + EPS)
        yhat = centred * inverse
        normed = (yhat * ln_gain).astype(jnp.bfloat16)
        preact = jnp.dot(normed, w_in, preferred_element_type=jnp.float32)
        activated = gelu_tanh(preact).astype(jnp.bfloat16)
        projected = jnp.dot(activated, w_out, preferred_element_type=jnp.float32)
        tangent_f = tangent.astype(jnp.float32)
        state = (cell_mask * (skip_rows.astype(jnp.float32) + layer_scale * projected)).astype(
            jnp.bfloat16
        )
        dproj = (cell_mask * layer_scale * tangent_f).astype(jnp.bfloat16)
        scale_part = jnp.sum(cell_mask * tangent_f * projected, axis=0)
        w_out_part = lax.dot_general(
            activated, dproj, (((0,), (0,)), ((), ())), preferred_element_type=jnp.float32
        )
        dactivated = lax.dot_general(
            dproj, w_out, (((1,), (1,)), ((), ())), preferred_element_type=jnp.float32
        )
        unused, pullback = jax.vjp(gelu_tanh, preact)
        dpreact = pullback(dactivated)[0].astype(jnp.bfloat16)
        w_in_part = lax.dot_general(
            normed, dpreact, (((0,), (0,)), ((), ())), preferred_element_type=jnp.float32
        )
        dnormed = lax.dot_general(
            dpreact, w_in, (((1,), (1,)), ((), ())), preferred_element_type=jnp.float32
        )
        gain_part = jnp.sum(dnormed * yhat, axis=0)
        dhat = dnormed * ln_gain
        conv_grad = inverse * (
            dhat
            - jnp.mean(dhat, axis=-1, keepdims=True)
            - yhat * jnp.mean(dhat * yhat, axis=-1, keepdims=True)
        )
        totals = (gain_part, w_in_part, w_out_part, scale_part)
        return (totals, (state, conv_grad.astype(jnp.bfloat16)))

    return block_step


def shards(fields, grad_out, block_count, ocean, kernel, ln_gain, w_in, w_out, layer_scale):
    samples, slot_count, tile_rows, tile_cols, channels = fields.shape
    half_kernel = KSIZE // 2
    half_axis = lax.axis_size("tiles") // 2
    top_bit = lax.axis_size("tiles").bit_length() - 2
    here = lax.axis_index("tiles")
    lower_half = here < half_axis
    at_start = here % half_axis == 0
    at_end = here % half_axis == half_axis - 1
    owned = block_count[0]
    strip_width = slot_count * tile_cols
    used_cols = owned * tile_cols
    slot_ids = jnp.arange(slot_count, dtype=jnp.int32)
    slot_mask = jnp.logical_and(slot_ids < owned, ocean > 0).astype(jnp.float32)
    masked = fields * slot_mask.astype(jnp.bfloat16)[None, :, None, None, None]
    strip = jnp.transpose(masked, (0, 2, 1, 3, 4)).reshape(
        samples, tile_rows, strip_width, channels
    )
    tangent = jnp.transpose(grad_out, (0, 2, 1, 3, 4)).reshape(
        samples, tile_rows, strip_width, channels
    )
    mask_strip = jnp.broadcast_to(
        slot_mask[None, None, :, None, None], (samples, tile_rows, slot_count, tile_cols, 1)
    ).reshape(samples, tile_rows, strip_width, 1)
    left_edge = strip[:, :, :half_kernel]
    right_edge = lax.dynamic_slice_in_dim(strip, used_cols - half_kernel, half_kernel, 2)
    up_send = jnp.where(lower_half, right_edge, left_edge)
    down_send = jnp.where(lower_half, left_edge, right_edge)
    from_lower = passed_along(up_send, "tiles", 1)
    from_upper = passed_along(down_send, "tiles", -1)
    far_edges = from_partner(jnp.stack([down_send, up_send]), "tiles", top_bit)
    from_lower = jnp.where(at_start, far_edges[0], from_lower)
    from_upper = jnp.where(at_end, far_edges[1], from_upper)
    from_west = jnp.where(lower_half, from_lower, from_upper)
    from_east = jnp.where(lower_half, from_upper, from_lower)
    blank_cols = jnp.zeros((samples, tile_rows, half_kernel, channels), jnp.bfloat16)
    extended = jnp.concatenate([from_west, strip, blank_cols], axis=2)
    extended = lax.dynamic_update_slice_in_dim(extended, from_east, used_cols + half_kernel, 2)
    mirrored = from_partner(extended[:, tile_rows - half_kernel :], "tiles", top_bit)
    north_rows = jnp.roll(mirrored[:, ::-1, ::-1], used_cols - strip_width, axis=2)
    south_rows = jnp.zeros(
        (samples, half_kernel, strip_width + 2 * half_kernel, channels), jnp.bfloat16
    )
    padded = jnp.concatenate([south_rows, extended, north_rows], axis=1)
    kernel_f = kernel.astype(jnp.float32)
    convolved = depthwise(padded, kernel_f, tile_rows, strip_width)
    block_step = make_block(ln_gain, w_in, w_out, layer_scale)
    start_totals = (
        jnp.zeros((channels,), jnp.float32),
        jnp.zeros((channels, HID), jnp.float32),
        jnp.zeros((HID, channels), jnp.float32),
        jnp.zeros((channels,), jnp.float32),
    )
    totals, outputs = block_step(
        start_totals,
        (
            convolved.reshape(-1, channels),
            strip.reshape(-1, channels),
            mask_strip.reshape(-1, 1),
            tangent.reshape(-1, channels),
        ),
    )
    gain_part, w_in_part, w_out_part, scale_part = totals
    conv_grad = outputs[1].reshape(samples, tile_rows, strip_width, channels)
    kernel_part = kernel_terms(conv_grad, padded, tile_rows, strip_width)
    dpadded = spread(conv_grad, kernel_f, tile_rows, strip_width)
    north_grad = dpadded[:, tile_rows + half_kernel :]
    returned = from_partner(
        jnp.roll(north_grad[:, ::-1, ::-1], used_cols - strip_width, axis=2).astype(jnp.bfloat16),
        "tiles",
        top_bit,
    ).astype(jnp.float32)
    dextended = dpadded[:, half_kernel : tile_rows + half_kernel]
    dextended = dextended.at[:, tile_rows - half_kernel :].add(returned)
    west_grad = dextended[:, :, :half_kernel]
    east_grad = lax.dynamic_slice_in_dim(dextended, used_cols + half_kernel, half_kernel, 2)
    core_grad = dextended[:, :, half_kernel : strip_width + half_kernel]
    up_grad = jnp.where(lower_half, east_grad, west_grad)
    down_grad = jnp.where(lower_half, west_grad, east_grad)
    grad_lower = passed_along(up_grad.astype(jnp.bfloat16), "tiles", 1).astype(up_grad.dtype)
    grad_upper = passed_along(down_grad.astype(jnp.bfloat16), "tiles", -1).astype(down_grad.dtype)
    far_grads = from_partner(
        jnp.stack([down_grad, up_grad]).astype(jnp.bfloat16), "tiles", top_bit
    ).astype(jnp.float32)
    grad_lower = jnp.where(at_start, far_grads[0], grad_lower)
    grad_upper = jnp.where(at_end, far_grads[1], grad_upper)
    to_head = jnp.where(lower_half, grad_lower, grad_upper)
    to_tail = jnp.where(lower_half, grad_upper, grad_lower)
    core_grad = core_grad.at[:, :, :half_kernel].add(to_head)
    tail_cols = (
        lax.dynamic_slice_in_dim(core_grad, used_cols - half_kernel, half_kernel, 2) + to_tail
    )
    core_grad = lax.dynamic_update_slice_in_dim(core_grad, tail_cols, used_cols - half_kernel, 2)
    grad_strip = (mask_strip * (tangent.astype(jnp.float32) + core_grad)).astype(jnp.bfloat16)
    kernel_sum, gain_sum, w_in_sum, w_out_sum, scale_sum = lax.psum(
        (kernel_part, gain_part, w_in_part, w_out_part, scale_part), ("tiles", "dp")
    )
    norm = (
        samples * lax.axis_size("dp") * slot_count * lax.axis_size("tiles") * tile_rows * tile_cols
    ) ** (-0.5)
    state_next = jnp.transpose(
        outputs[0].reshape(samples, tile_rows, slot_count, tile_cols, channels), (0, 2, 1, 3, 4)
    )
    grad_fields = jnp.transpose(
        grad_strip.reshape(samples, tile_rows, slot_count, tile_cols, channels), (0, 2, 1, 3, 4)
    )
    return (
        state_next,
        grad_fields,
        kernel_sum * norm,
        gain_sum * norm,
        w_in_sum * norm,
        w_out_sum * norm,
        scale_sum * norm,
    )


def solution(mesh):
    placed = (
        P("dp", "tiles", None, None, None),
        P("dp", "tiles", None, None, None),
        P("tiles"),
        P("tiles"),
        P(),
        P(),
        P(),
        P(),
        P(),
    )
    return jax.shard_map(
        shards,
        mesh=mesh,
        in_specs=placed,
        out_specs=(
            P("dp", "tiles", None, None, None),
            P("dp", "tiles", None, None, None),
            P(),
            P(),
            P(),
            P(),
            P(),
        ),
        check_vma=False,
    )
```

profile of v0, /device:TPU:1, one launch (start us, length us, event | category | flops | bytes accessed | tf_op | source)
XLA Modules:
  0.0 466.2 jit_solution(11141867226133254844)
XLA Ops:
  9.7 5.6 %collective-permute-start.1 = (bf16[1,16,3,256]{3,2,1,0:T(4,128)(2,1)S(1)}, bf16[1,16,3,256]{3,2,1,0:T(4,128)(2,1)S(1)}, u32[]{:S(2)}, u32[]{:S(2)}) collective-permute-start(bf16[1,16,3,256]{3,2,1,0:T(4,128)(2,1)S(1)} %get-tuple-element.105), channel_id=1, source_target_pairs={{0,2},{2,4},{4,6},{6,8},{8,10},{10,12},{12,14},{14,16},{16,18},{18... | collective-permute-start | bytes 73736 | tf_op jit(solution)/shard_map/ppermute | solution.py:16
  15.4 4.5 collective-permute-start.2
  19.9 2.1 collective-permute-start
  24.3 2.2 collective-permute-done
  27.0 2.5 collective-permute-start.3
  31.5 3.2 collective-permute-done.3
  34.9 8.2 %fusion.237 = (f32[16,48]{1,0:T(8,128)S(1)}, f32[1,16,48,256]{3,2,1,0:T(8,128)S(1)}) fusion(bf16[1,3,54,256]{3,2,1,0:T(8,128)(2,1)S(1)} %fusion.232, bf16[1,16,54,256]{3,2,1,0:T(8,128)(2,1)S(1)} %dynamic_update_slice.6, f32[256]{0:T(256)S(1)} %bitcast.319, f32[256]{0:T(256)S(1)} %bitcast.317, f32[256]{0:T(256)S(1)} %bitcast.315, f32[256]{0:T(256)S(1)} %bitcast.313, ...), kind=kLoop, calls=%fused_computation.458 | loop fusion | flops 41286912 | bytes 4136960 | tf_op jit(solution)/shard_map/reduce_sum | solution.py:83
  45.3 2.0 fusion.207
  47.3 1.6 fusion.244
  48.9 2.4 fusion.6
  51.4 1.6 fusion.243
  53.0 2.1 multiply_reduce_fusion
  55.5 1.6 fusion.198
  59.6 1.7 fusion.179
  62.0 103.7 %all-reduce.2 = (f32[7,7,256]{2,1,0:T(8,128)S(1)}, f32[256]{0:T(256)S(1)}, f32[256]{0:T(256)S(1)}) all-reduce(f32[7,7,256]{2,1,0:T(8,128)S(1)} %constant_dynamic-update-slice_fusion, f32[256]{0:T(256)S(1)} %copy-done.49, f32[256]{0:T(256)S(1)} %copy-done.48), channel_id=1, replica_groups=mesh['tiles'=256,'dp'=2] {'tiles','dp'}, use_global_device_ids=true, to_apply=%region_53.54 | all-reduce | flops 13056 | bytes 104448 | tf_op jit(solution)/shard_map/psum | solution.py:219
  166.5 10.0 %fusion.100 = f32[1,22,54,256]{3,2,1,0:T(8,128)S(1)} fusion(f32[1,16,48,256]{3,2,1,0:T(8,128)S(1)} %convert.16, f32[256]{0:T(256)S(1)} %bitcast.320, f32[256]{0:T(256)S(1)} %bitcast.318, f32[256]{0:T(256)S(1)} %bitcast.316, f32[256]{0:T(256)S(1)} %bitcast.314, f32[256]{0:T(256)S(1)} %bitcast.312, f32[256]{0:T(256)S(1)} %bitcast.310, f32[256]{0:T(256)S(1)} %bitcast.308, ...), kind=kLoop, calls=%fused_computation.221 | loop fusion | flops 29500416 | bytes 2053120 | tf_op jit(solution)/shard_map/add | solution.py:75
  176.8 2.5 collective-permute-start.4
  180.0 3.6 collective-permute-done.4
  183.6 6.0 %collective-permute-start.6 = (bf16[1,16,3,256]{3,2,1,0:T(4,128)(2,1)S(1)}, bf16[1,16,3,256]{3,2,1,0:T(4,128)(2,1)S(1)}, u32[]{:S(2)}, u32[]{:S(2)}) collective-permute-start(bf16[1,16,3,256]{3,2,1,0:T(4,128)(2,1)S(1)} %get-tuple-element.100), channel_id=1, source_target_pairs={{0,2},{2,4},{4,6},{6,8},{8,10},{10,12},{12,14},{14,16},{16,18},{18... | collective-permute-start | bytes 73736 | tf_op jit(solution)/shard_map/ppermute | solution.py:16
  189.6 1.9 collective-permute-start.7
  191.6 2.5 collective-permute-start.5
  195.5 2.7 collective-permute-done.5
  199.8 256.1 %all-reduce.6.cloned.1.call-done = (f32[256,1024]{1,0:T(8,128)}, f32[1024,256]{1,0:T(8,128)}) async-done(((f32[256,1024]{1,0:T(8,128)}, f32[1024,256]{1,0:T(8,128)}), (f32[256,1024]{1,0:T(8,128)}, f32[1024,256]{1,0:T(8,128)})) %all-reduce.6.cloned.1.call-update) | async-done | bytes 2097168 | tf_op jit(solution)/shard_map/psum | solution.py:219
  455.9 2.4 broadcast_multiply_fusion
  (175 shorter events, 17.8 us)
Async XLA Ops:
  7.2 448.7 %all-reduce.6.cloned.1.call-start = ((), (), s32[]{:S(2)}) async-start(), calls=%async_computation | async-start | bytes 4194304 | tf_op jit(solution)/shard_map/psum | solution.py:219
  9.7 14.5 %collective-permute-start.1 = (bf16[1,16,3,256]{3,2,1,0:T(4,128)(2,1)S(1)}, bf16[1,16,3,256]{3,2,1,0:T(4,128)(2,1)S(1)}, u32[]{:S(2)}, u32[]{:S(2)}) collective-permute-start(bf16[1,16,3,256]{3,2,1,0:T(4,128)(2,1)S(1)} %get-tuple-element.105), channel_id=1, source_target_pairs={{0,2},{2,4},{4,6},{6,8},{8,10},{10,12},{12,14},{14,16},{16,18},{18... | collective-permute-start | bytes 73736 | tf_op jit(solution)/shard_map/ppermute | solution.py:16
  15.4 8.9 %collective-permute-start.2 = (bf16[1,16,3,256]{3,2,1,0:T(4,128)(2,1)S(1)}, bf16[1,16,3,256]{3,2,1,0:T(4,128)(2,1)S(1)}, u32[]{:S(2)}, u32[]{:S(2)}) collective-permute-start(bf16[1,16,3,256]{3,2,1,0:T(4,128)(2,1)S(1)} %get-tuple-element.104), channel_id=1, source_target_pairs={{2,0},{4,2},{6,4},{8,6},{10,8},{12,10},{14,12},{16,14},{18,16},{20... | collective-permute-start | bytes 73736 | tf_op jit(solution)/shard_map/ppermute | solution.py:16
  19.9 6.5 %collective-permute-start = (bf16[2,1,16,3,256]{4,3,2,1,0:T(4,128)(2,1)S(1)}, bf16[2,1,16,3,256]{4,3,2,1,0:T(4,128)(2,1)S(1)}, u32[]{:S(2)}, u32[]{:S(2)}) collective-permute-start(bf16[2,1,16,3,256]{4,3,2,1,0:T(4,128)(2,1)S(1)} %pad_maximum_fusion.1), channel_id=1, source_target_pairs={{0,256},{256,0},{2,258},{258,2},{4,260},{260,4},{6,262},{262,6},{8... | collective-permute-start | bytes 147464 | tf_op jit(solution)/shard_map/ppermute | solution.py:26
  27.0 7.7 %collective-permute-start.3 = (bf16[1,3,54,256]{3,2,1,0:T(8,128)(2,1)S(1)}, bf16[1,3,54,256]{3,2,1,0:T(8,128)(2,1)S(1)}, u32[]{:S(2)}, u32[]{:S(2)}) collective-permute-start(bf16[1,3,54,256]{3,2,1,0:T(8,128)(2,1)S(1)} %slice.869), channel_id=1, source_target_pairs={{0,256},{256,0},{2,258},{258,2},{4,260},{260,4},{6,262},{262,6},{8... | collective-permute-start | bytes 248840 | tf_op jit(solution)/shard_map/ppermute | solution.py:26
  61.3 105.0 %copy-start.6 = (f32[1,1,256]{2,1,0:T(1,128)S(1)}, f32[1,1,256]{2,1,0:T(1,128)}, u32[]{:S(2)}) copy-start(f32[1,1,256]{2,1,0:T(1,128)} %copy-done.5) | copy-start | bytes 3076
  61.3 105.0 %copy-start.8 = (f32[1,1,256]{2,1,0:T(1,128)S(1)}, f32[1,1,256]{2,1,0:T(1,128)}, u32[]{:S(2)}) copy-start(f32[1,1,256]{2,1,0:T(1,128)} %copy-done.7) | copy-start | bytes 3076
  61.4 105.0 %copy-start.10 = (f32[1,1,256]{2,1,0:T(1,128)S(1)}, f32[1,1,256]{2,1,0:T(1,128)}, u32[]{:S(2)}) copy-start(f32[1,1,256]{2,1,0:T(1,128)} %copy-done.9) | copy-start | bytes 3076
  61.4 105.0 %copy-start.12 = (f32[1,1,256]{2,1,0:T(1,128)S(1)}, f32[1,1,256]{2,1,0:T(1,128)}, u32[]{:S(2)}) copy-start(f32[1,1,256]{2,1,0:T(1,128)} %copy-done.11) | copy-start | bytes 3076
  61.4 105.0 %copy-start.14 = (f32[1,1,256]{2,1,0:T(1,128)S(1)}, f32[1,1,256]{2,1,0:T(1,128)}, u32[]{:S(2)}) copy-start(f32[1,1,256]{2,1,0:T(1,128)} %copy-done.13) | copy-start | bytes 3076
  61.4 105.0 %copy-start.16 = (f32[1,1,256]{2,1,0:T(1,128)S(1)}, f32[1,1,256]{2,1,0:T(1,128)}, u32[]{:S(2)}) copy-start(f32[1,1,256]{2,1,0:T(1,128)} %copy-done.15) | copy-start | bytes 3076
  61.4 105.0 %copy-start.18 = (f32[1,1,256]{2,1,0:T(1,128)S(1)}, f32[1,1,256]{2,1,0:T(1,128)}, u32[]{:S(2)}) copy-start(f32[1,1,256]{2,1,0:T(1,128)} %copy-done.17) | copy-start | bytes 3076
  61.4 105.0 %copy-start.20 = (f32[1,1,256]{2,1,0:T(1,128)S(1)}, f32[1,1,256]{2,1,0:T(1,128)}, u32[]{:S(2)}) copy-start(f32[1,1,256]{2,1,0:T(1,128)} %copy-done.19) | copy-start | bytes 3076
  61.4 105.0 %copy-start.22 = (f32[1,1,256]{2,1,0:T(1,128)S(1)}, f32[1,1,256]{2,1,0:T(1,128)}, u32[]{:S(2)}) copy-start(f32[1,1,256]{2,1,0:T(1,128)} %copy-done.21) | copy-start | bytes 3076
  61.4 105.0 %copy-start.24 = (f32[1,1,256]{2,1,0:T(1,128)S(1)}, f32[1,1,256]{2,1,0:T(1,128)}, u32[]{:S(2)}) copy-start(f32[1,1,256]{2,1,0:T(1,128)} %copy-done.23) | copy-start | bytes 3076
  61.4 105.0 %copy-start.26 = (f32[1,1,256]{2,1,0:T(1,128)S(1)}, f32[1,1,256]{2,1,0:T(1,128)}, u32[]{:S(2)}) copy-start(f32[1,1,256]{2,1,0:T(1,128)} %copy-done.25) | copy-start | bytes 3076
  61.4 105.0 %copy-start.28 = (f32[1,1,256]{2,1,0:T(1,128)S(1)}, f32[1,1,256]{2,1,0:T(1,128)}, u32[]{:S(2)}) copy-start(f32[1,1,256]{2,1,0:T(1,128)} %copy-done.27) | copy-start | bytes 3076
  61.5 105.0 %copy-start.30 = (f32[1,1,256]{2,1,0:T(1,128)S(1)}, f32[1,1,256]{2,1,0:T(1,128)}, u32[]{:S(2)}) copy-start(f32[1,1,256]{2,1,0:T(1,128)} %copy-done.29) | copy-start | bytes 3076
  61.5 105.0 %copy-start.32 = (f32[1,1,256]{2,1,0:T(1,128)S(1)}, f32[1,1,256]{2,1,0:T(1,128)}, u32[]{:S(2)}) copy-start(f32[1,1,256]{2,1,0:T(1,128)} %copy-done.31) | copy-start | bytes 3076
  61.5 105.0 %copy-start.34 = (f32[1,1,256]{2,1,0:T(1,128)S(1)}, f32[1,1,256]{2,1,0:T(1,128)}, u32[]{:S(2)}) copy-start(f32[1,1,256]{2,1,0:T(1,128)} %copy-done.33) | copy-start | bytes 3076
  176.8 6.7 %collective-permute-start.4 = (bf16[1,3,54,256]{3,2,1,0:T(8,128)(2,1)S(1)}, bf16[1,3,54,256]{3,2,1,0:T(8,128)(2,1)S(1)}, u32[]{:S(2)}, u32[]{:S(2)}) collective-permute-start(bf16[1,3,54,256]{3,2,1,0:T(8,128)(2,1)S(1)} %fusion.230), channel_id=1, source_target_pairs={{0,256},{256,0},{2,258},{258,2},{4,260},{260,4},{6,262},{262,6},{8... | collective-permute-start | bytes 248840 | tf_op jit(solution)/shard_map/ppermute | solution.py:26
  183.6 14.6 %collective-permute-start.6 = (bf16[1,16,3,256]{3,2,1,0:T(4,128)(2,1)S(1)}, bf16[1,16,3,256]{3,2,1,0:T(4,128)(2,1)S(1)}, u32[]{:S(2)}, u32[]{:S(2)}) collective-permute-start(bf16[1,16,3,256]{3,2,1,0:T(4,128)(2,1)S(1)} %get-tuple-element.100), channel_id=1, source_target_pairs={{0,2},{2,4},{4,6},{6,8},{8,10},{10,12},{12,14},{14,16},{16,18},{18... | collective-permute-start | bytes 73736 | tf_op jit(solution)/shard_map/ppermute | solution.py:16
  189.6 8.6 %collective-permute-start.7 = (bf16[1,16,3,256]{3,2,1,0:T(4,128)(2,1)S(1)}, bf16[1,16,3,256]{3,2,1,0:T(4,128)(2,1)S(1)}, u32[]{:S(2)}, u32[]{:S(2)}) collective-permute-start(bf16[1,16,3,256]{3,2,1,0:T(4,128)(2,1)S(1)} %get-tuple-element.99), channel_id=1, source_target_pairs={{2,0},{4,2},{6,4},{8,6},{10,8},{12,10},{14,12},{16,14},{18,16},{20... | collective-permute-start | bytes 73736 | tf_op jit(solution)/shard_map/ppermute | solution.py:16
  191.6 6.6 %collective-permute-start.5 = (bf16[2,1,16,3,256]{4,3,2,1,0:T(4,128)(2,1)S(1)}, bf16[2,1,16,3,256]{4,3,2,1,0:T(4,128)(2,1)S(1)}, u32[]{:S(2)}, u32[]{:S(2)}) collective-permute-start(bf16[2,1,16,3,256]{4,3,2,1,0:T(4,128)(2,1)S(1)} %pad_maximum_fusion.2), channel_id=1, source_target_pairs={{0,256},{256,0},{2,258},{258,2},{4,260},{260,4},{6,262},{262,6},{8... | collective-permute-start | bytes 147464 | tf_op jit(solution)/shard_map/ppermute | solution.py:26
  (37 other events, 912.1 us)
Sparse Core Ops, SparseCore 0:
  180.1 275.7 all-reduce.5
where the time goes:
time: 467 us; the launch traced here: 466 us
  waiting for transfers between devices  268 us (57%)
  blocking collectives  104 us (22%)
  other arithmetic  33.2 us (7%)
  starting transfers between devices  27.6 us (6%)
  between operations  15.9 us (3%)
  matrix products  10.9 us (2%)
  local copies, waits for them, and re-layouts  7.34 us (2%)
    psum x1, waiting for transfers between devices, shards(): lax.psum((kernel_part, gain_part, w_in_part, w_out_part, scale_part), ('t...  256 us
    psum x1, blocking collectives, shards(): lax.psum((kernel_part, gain_part, w_in_part, w_out_part, scale_part), ('t...  104 us
    ppermute x4, starting transfers between devices, passed_along(): return lax.ppermute(block, axis, route)  18 us
    ppermute x4, waiting for transfers between devices, from_partner(): return lax.ppermute(block, axis, route)  11.6 us
    add x1, other arithmetic, spread(): running = running + kernel_f[row_shift, col_shift] * window  10 us
    ppermute x4, starting transfers between devices, from_partner(): return lax.ppermute(block, axis, route)  9.62 us
  transfers between devices with their start and end apart: 9, of which 5 were waited for; matrix products, arithmetic and copies ran while one was open for 2% of the time, Pallas kernels for 0%

commit v1 on v0

--- a/solution.py
+++ b/solution.py
@@ -1,10 +1,285 @@
+import functools
+
 import jax
 import jax.numpy as jnp
 from jax import lax
+from jax.experimental import pallas as pl
+from jax.experimental.pallas import tpu as pltpu
 from jax.sharding import PartitionSpec as P
 
 HID = 1024
 KSIZE = 7
+NX, NZ, NYH = 4, 8, 4
+NY = 2 * NYH
+GROUP_X, GROUP_Y, GROUP_Z = 1024, 512, 512
+HALF = GROUP_X + GROUP_Y + GROUP_Z
+SMALL = 64
+XR, YR, ZR = GROUP_X // NX, GROUP_Y // NY, GROUP_Z // NZ
+XA, XB = XR // 2 // NY, XR // 2 // NZ
+YX, ZX = YR // NX, ZR // NX
+SR = SMALL // NY
+F32, BF16 = jnp.float32, jnp.bfloat16
+
+
+class Place:
+    def __init__(self):
+        t = lax.axis_index("tiles")
+        self.t = t
+        self.lo = lax.axis_index("dp")
+        self.core = t % 2
+        self.yh = (t // 2) % NYH
+        self.z = (t // (2 * NYH)) % NZ
+        self.x = t // (2 * NYH * NZ)
+        self.y = self.yh * 2 + self.lo
+
+    def along(self, axis, step):
+        if axis == "core":
+            place = 1 - self.core
+            return place, (self.t + place - self.core, self.lo)
+        if axis == "x":
+            place = (self.x + step) % NX
+            return place, (self.t + (place - self.x) * (2 * NYH * NZ), self.lo)
+        if axis == "z":
+            place = (self.z + step) % NZ
+            return place, (self.t + (place - self.z) * (2 * NYH), self.lo)
+        place = (self.y + step) % NY
+        return place, (self.t + (place // 2 - self.yh) * 2, place % 2)
+
+
+COUNT = {"x": NX, "y": NY, "z": NZ, "core": 2}
+
+
+def steps(axis):
+    n = COUNT[axis]
+    near = []
+    for d in range(1, n // 2 + 1):
+        near += [d, n - d] if d != n - d else [d]
+    return near
+
+
+def send(src, dst, send_sem, recv_sem, device):
+    pltpu.make_async_remote_copy(
+        src_ref=src,
+        dst_ref=dst,
+        send_sem=send_sem,
+        recv_sem=recv_sem,
+        device_id=device,
+        device_id_type=pl.DeviceIdType.MESH,
+    ).start()
+
+
+def await_bytes(like, sem):
+    pltpu.make_async_copy(like, like, sem).wait()
+
+
+def rows(start, size):
+    return pl.ds(pl.multiple_of(start, size), size)
+
+
+def reduce_kernel(
+    wide, small, out, small_out, core_out, core_in, held, x_in, y_in, z_in, p_out, xa_in, xb_in,
+    w_out, w_in, zz, yy, s_core, s_y, s_z, s_x, s_held, ss, rs
+):
+    here = Place()
+    c, x, y, z = here.core, here.x, here.y, here.z
+    me = {"x": x, "y": y, "z": z}
+    barrier = pltpu.get_barrier_semaphore()
+    greeted = 0
+    for axis in ("core", "x", "y", "z"):
+        for d in steps(axis):
+            pl.semaphore_signal(
+                barrier, inc=1, device_id=here.along(axis, d)[1], device_id_type=pl.DeviceIdType.MESH
+            )
+            greeted += 1
+    pl.semaphore_wait(barrier, greeted)
+    Y0, Z0 = GROUP_X, GROUP_X + GROUP_Y
+    regions = [(0, GROUP_X), (Y0, GROUP_Y), (Z0, GROUP_Z)]
+    partner = here.along("core", 1)[1]
+
+    send(small.at[1 - c], s_core, ss.at[3], rs.at[3], partner)
+    for i in (1, 2, 0):
+        start, size = regions[i]
+        core_out[pl.ds(start, size)] = wide[1 - c, pl.ds(start, size)].astype(BF16)
+        span = pl.ds(start, size)
+        send(core_out.at[span], core_in.at[span], ss.at[i], rs.at[i], partner)
+
+    await_bytes(s_core, rs.at[3])
+    s_held[...] = small[c] + s_core[...]
+    for d in steps("y"):
+        place, device = here.along("y", d)
+        send(s_held.at[rows(place * SR, SR)], s_y.at[d - 1], ss.at[7], rs.at[7], device)
+    for i, axis, size, landing in ((1, "y", YR, y_in), (2, "z", ZR, z_in), (0, "x", XR, x_in)):
+        start, extent = regions[i]
+        span = pl.ds(start, extent)
+        await_bytes(core_in.at[span], rs.at[i])
+        held[span] = (wide[c, span] + core_in[span].astype(F32)).astype(BF16)
+        for d in steps(axis):
+            place, device = here.along(axis, d)
+            send(
+                held.at[rows(start + place * size, size)], landing.at[d - 1], ss.at[4 + i], rs.at[4 + i], device
+            )
+
+    def own(start, size):
+        span = rows(start, size)
+        return wide[c, span] + core_in[span].astype(F32)
+
+    def total(first, landing):
+        for k in range(landing.shape[0]):
+            first = first + landing[k].astype(F32)
+        return first
+
+    await_bytes(s_y, rs.at[7])
+    s_own = total(s_held[rows(y * SR, SR)], s_y)
+    s_z[z] = s_own
+    for d in steps("z"):
+        send(s_z.at[z], s_z.at[z], ss.at[11], rs.at[11], here.along("z", d)[1])
+    await_bytes(y_in, rs.at[5])
+    y_own = total(own(Y0 + y * YR, YR), y_in)
+    for k in range(NX):
+        w_out[k, :YX] = y_own[k * YX : (k + 1) * YX].astype(BF16)
+    await_bytes(z_in, rs.at[6])
+    z_own = total(own(Z0 + z * ZR, ZR), z_in)
+    for k in range(NX):
+        w_out[k, YX:] = z_own[k * ZX : (k + 1) * ZX].astype(BF16)
+    for d in steps("x"):
+        place, device = here.along("x", d)
+        send(w_out.at[place], w_in.at[d - 1], ss.at[10], rs.at[10], device)
+    await_bytes(x_in, rs.at[4])
+    p_own = total(own(x * XR, XR), x_in)
+    p_out[...] = p_own.astype(BF16)
+    for d in steps("y"):
+        place, device = here.along("y", d)
+        send(p_out.at[rows(place * XA, XA)], xa_in.at[d - 1], ss.at[8], rs.at[8], device)
+    for d in steps("z"):
+        place, device = here.along("z", d)
+        send(p_out.at[rows(XR // 2 + place * XB, XB)], xb_in.at[d - 1], ss.at[9], rs.at[9], device)
+
+    await_bytes(s_z.at[pl.ds(0, NZ - 1)], rs.at[11])
+    s_x[x] = jnp.sum(s_z[...], axis=0)
+    for d in steps("x"):
+        send(s_x.at[x], s_x.at[x], ss.at[14], rs.at[14], here.along("x", d)[1])
+
+    await_bytes(w_in, rs.at[10])
+    mine = w_out[x].astype(F32)
+    mine = total(mine, w_in)
+    await_bytes(xa_in, rs.at[8])
+    zz[z, :XA] = total(p_out[rows(y * XA, XA)].astype(F32), xa_in).astype(BF16)
+    zz[z, XA:] = mine[:YX].astype(BF16)
+    for d in steps("z"):
+        send(zz.at[z], zz.at[z], ss.at[12], rs.at[12], here.along("z", d)[1])
+    await_bytes(xb_in, rs.at[9])
+    yy[y, :XB] = total(p_out[rows(XR // 2 + z * XB, XB)].astype(F32), xb_in).astype(BF16)
+    yy[y, XB:] = mine[YX:].astype(BF16)
+    for d in steps("y"):
+        send(yy.at[y], yy.at[y], ss.at[13], rs.at[13], here.along("y", d)[1])
+
+    def line_total(landing, count):
+        run = landing[0].astype(F32)
+        for k in range(1, count):
+            run = run + landing[k].astype(F32)
+        return run
+
+    await_bytes(s_x.at[pl.ds(0, NX - 1)], rs.at[14])
+    small_out[c, rows(y * SR, SR)] = jnp.sum(s_x[...], axis=0)
+
+    def spread_out(ref, axis, sem):
+        for d in steps(axis):
+            send(ref, ref, ss.at[sem], rs.at[sem], here.along(axis, d)[1])
+
+    spread_out(small_out.at[c, rows(y * SR, SR)], "y", 15)
+    await_bytes(zz.at[pl.ds(0, NZ - 1)], rs.at[12])
+    zsum = line_total(zz, NZ).astype(BF16)
+    out[c, rows(x * XR + y * XA, XA)] = zsum[:XA]
+    out[c, rows(Y0 + y * YR + x * YX, YX)] = zsum[XA:]
+    spread_out(out.at[c, rows(x * XR + y * XA, XA)], "y", 16)
+    spread_out(out.at[c, rows(Y0 + y * YR + x * YX, YX)], "x", 17)
+    await_bytes(yy.at[pl.ds(0, NY - 1)], rs.at[13])
+    ysum = line_total(yy, NY).astype(BF16)
+    out[c, rows(x * XR + XR // 2 + z * XB, XB)] = ysum[:XB]
+    out[c, rows(Z0 + z * ZR + x * ZX, ZX)] = ysum[XB:]
+    spread_out(out.at[c, rows(x * XR + XR // 2 + z * XB, XB)], "z", 18)
+    spread_out(out.at[c, rows(Z0 + z * ZR + x * ZX, ZX)], "x", 19)
+
+    await_bytes(out.at[0, pl.ds(0, (NX - 1) * YX)], rs.at[17])
+    spread_out(out.at[c, rows(Y0 + y * YR, YR)], "y", 20)
+    await_bytes(out.at[0, pl.ds(0, (NX - 1) * ZX)], rs.at[19])
+    spread_out(out.at[c, rows(Z0 + z * ZR, ZR)], "z", 21)
+    await_bytes(out.at[0, pl.ds(0, (NY - 1) * XA)], rs.at[16])
+    await_bytes(out.at[0, pl.ds(0, (NZ - 1) * XB)], rs.at[18])
+    spread_out(out.at[c, rows(x * XR, XR)], "x", 22)
+
+    await_bytes(small_out.at[0, pl.ds(0, (NY - 1) * SR)], rs.at[15])
+    send(small_out.at[c], small_out.at[c], ss.at[23], rs.at[23], partner)
+    for i, sem, got in ((1, 20, (NY - 1) * YR), (2, 21, (NZ - 1) * ZR), (0, 22, (NX - 1) * XR)):
+        await_bytes(out.at[0, pl.ds(0, got)], rs.at[sem])
+        ref = out.at[c, pl.ds(*regions[i])]
+        send(ref, ref, ss.at[24 + i], rs.at[24 + i], partner)
+    await_bytes(small_out.at[0], rs.at[23])
+    for i in range(3):
+        await_bytes(out.at[0, pl.ds(*regions[i])], rs.at[24 + i])
+
+    for i in range(3):
+        await_bytes(core_out.at[pl.ds(*regions[i])], ss.at[i])
+        await_bytes(out.at[0, pl.ds(*regions[i])], ss.at[24 + i])
+    await_bytes(s_core, ss.at[3])
+    await_bytes(x_in, ss.at[4])
+    await_bytes(y_in, ss.at[5])
+    await_bytes(z_in, ss.at[6])
+    await_bytes(s_y, ss.at[7])
+    await_bytes(xa_in, ss.at[8])
+    await_bytes(xb_in, ss.at[9])
+    await_bytes(w_in, ss.at[10])
+    await_bytes(s_z.at[pl.ds(0, NZ - 1)], ss.at[11])
+    await_bytes(zz.at[pl.ds(0, NZ - 1)], ss.at[12])
+    await_bytes(yy.at[pl.ds(0, NY - 1)], ss.at[13])
+    await_bytes(s_x.at[pl.ds(0, NX - 1)], ss.at[14])
+    await_bytes(small_out.at[0, pl.ds(0, (NY - 1) * SR)], ss.at[15])
+    await_bytes(out.at[0, pl.ds(0, (NY - 1) * XA)], ss.at[16])
+    await_bytes(out.at[0, pl.ds(0, (NX - 1) * YX)], ss.at[17])
+    await_bytes(out.at[0, pl.ds(0, (NZ - 1) * XB)], ss.at[18])
+    await_bytes(out.at[0, pl.ds(0, (NX - 1) * ZX)], ss.at[19])
+    await_bytes(out.at[0, pl.ds(0, (NY - 1) * YR)], ss.at[20])
+    await_bytes(out.at[0, pl.ds(0, (NZ - 1) * ZR)], ss.at[21])
+    await_bytes(out.at[0, pl.ds(0, (NX - 1) * XR)], ss.at[22])
+    await_bytes(small_out.at[0], ss.at[23])
+
+
+def reduce_all(wide, small):
+    vmem = pl.BlockSpec(memory_space=pltpu.VMEM)
+    return pl.pallas_call(
+        reduce_kernel,
+        out_shape=(
+            jax.ShapeDtypeStruct((2, HALF, 128), BF16),
+            jax.ShapeDtypeStruct((2, SMALL, 128), F32),
+        ),
+        in_specs=[vmem, vmem],
+        out_specs=(vmem, vmem),
+        scratch_shapes=[
+            pltpu.VMEM((HALF, 128), BF16),
+            pltpu.VMEM((HALF, 128), BF16),
+            pltpu.VMEM((HALF, 128), BF16),
+            pltpu.VMEM((NX - 1, XR, 128), BF16),
+            pltpu.VMEM((NY - 1, YR, 128), BF16),
+            pltpu.VMEM((NZ - 1, ZR, 128), BF16),
+            pltpu.VMEM((XR, 128), BF16),
+            pltpu.VMEM((NY - 1, XA, 128), BF16),
+            pltpu.VMEM((NZ - 1, XB, 128), BF16),
+            pltpu.VMEM((NX, YX + ZX, 128), BF16),
+            pltpu.VMEM((NX - 1, YX + ZX, 128), BF16),
+            pltpu.VMEM((NZ, XA + YX, 128), BF16),
+            pltpu.VMEM((NY, XB + ZX, 128), BF16),
+            pltpu.VMEM((SMALL, 128), F32),
+            pltpu.VMEM((NY - 1, SR, 128), F32),
+            pltpu.VMEM((NZ, SR, 128), F32),
+            pltpu.VMEM((NX, SR, 128), F32),
+            pltpu.VMEM((SMALL, 128), F32),
+            pltpu.SemaphoreType.DMA((27,)),
+            pltpu.SemaphoreType.DMA((27,)),
+        ],
+        compiler_params=pltpu.CompilerParams(
+            collective_id=1, has_side_effects=True, vmem_limit_bytes=32 * 1024 * 1024
+        ),
+    )(wide, small)
 
 
 EPS = 1e-06
@@ -216,9 +491,32 @@
     )
     core_grad = lax.dynamic_update_slice_in_dim(core_grad, tail_cols, used_cols - half_kernel, 2)
     grad_strip = (mask_strip * (tangent.astype(jnp.float32) + core_grad)).astype(jnp.bfloat16)
-    kernel_sum, gain_sum, w_in_sum, w_out_sum, scale_sum = lax.psum(
-        (kernel_part, gain_part, w_in_part, w_out_part, scale_part), ("tiles", "dp")
-    )
+    wide = jnp.stack(
+        [
+            jnp.transpose(w_in_part.reshape(channels, -1, 128), (1, 0, 2)).reshape(HALF, 128),
+            jnp.transpose(w_out_part.reshape(-1, channels // 128, 128), (1, 0, 2)).reshape(HALF, 128),
+        ]
+    )
+    taps = KSIZE * KSIZE
+    small = jnp.concatenate(
+        [
+            kernel_part.reshape(taps, channels),
+            gain_part[None],
+            scale_part[None],
+            jnp.zeros((SMALL - taps - 2, channels), F32),
+        ]
+    )
+    small = jnp.stack([small[:, :128], small[:, 128:]])
+    wide, small = reduce_all(wide, small)
+    w_in_sum = jnp.transpose(
+        wide[0].reshape(-1, channels, 128), (1, 0, 2)
+    ).reshape(channels, HID).astype(F32)
+    w_out_sum = jnp.transpose(
+        wide[1].reshape(channels // 128, HID, 128), (1, 0, 2)
+    ).reshape(HID, channels).astype(F32)
+    small = jnp.concatenate([small[0], small[1]], axis=1)
+    kernel_sum = small[:taps].reshape(KSIZE, KSIZE, channels)
+    gain_sum, scale_sum = small[taps], small[taps + 1]
     norm = (
         samples * lax.axis_size("dp") * slot_count * lax.axis_size("tiles") * tile_rows * tile_cols
     ) ** (-0.5)

time: 467 us -> 159 us (0.34)
  waiting for transfers between devices: 268 us -> 4.36 us
  blocking collectives: 104 us -> 0 us
  Pallas kernels: 0 us -> 41.4 us
  local copies, waits for them, and re-layouts: 7.34 us -> 26.8 us
  between operations: 15.9 us -> 1.94 us
  other arithmetic: 33.2 us -> 39.3 us
    psum x1 -> x0, waiting for transfers between devices: 256 us -> none  [shards(): lax.psum((kernel_part, gain_part, w_in_part, w_out_part, scale_part), ('t...]
    psum x1 -> x0, blocking collectives: 104 us -> none  [shards(): lax.psum((kernel_part, gain_part, w_in_part, w_out_part, scale_part), ('t...]
    pallas_call x0 -> x1, Pallas kernels: none -> 41.4 us  [reduce_all(): pl.pallas_call(reduce_kernel, out_shape=(jax.ShapeDtypeStruct((2, HALF, 1...]
    ppermute x4, waiting for transfers between devices: 11.6 us -> 4.35 us  [from_partner(): return lax.ppermute(block, axis, route)]
    ppermute x4, starting transfers between devices: 9.62 us -> 14.6 us  [from_partner(): return lax.ppermute(block, axis, route)]
    another operation x7, local copies, waits for them, and re-layouts: 0.2 us -> 5.01 us  [kernel_terms(): stacked.append(jnp.stack(taps))]
  transfers between devices with their start and end apart: 9 -> 8, of which waited for: 5 -> 2; matrix products, arithmetic and copies ran while one was open for 2% -> 9% of each run, Pallas kernels for 0% -> 0%
where the time goes in v1:
time: 159 us; the launch traced here: 158 us
  Pallas kernels  41.4 us (26%)
  other arithmetic  39.3 us (25%)
  starting transfers between devices  31.9 us (20%)
  local copies, waits for them, and re-layouts  26.8 us (17%)
  matrix products  11.9 us (7%)
  waiting for transfers between devices  4.36 us (3%)
  between operations  1.94 us (1%)
    pallas_call x1, Pallas kernels, reduce_all(): pl.pallas_call(reduce_kernel, out_shape=(jax.ShapeDtypeStruct((2, HALF, 1...  41.4 us
    ppermute x4, starting transfers between devices, passed_along(): return lax.ppermute(block, axis, route)  17.3 us
    ppermute x4, starting transfers between devices, from_partner(): return lax.ppermute(block, axis, route)  14.6 us
    add x1, other arithmetic, spread(): running = running + kernel_f[row_shift, col_shift] * window  10 us
    reduce_sum x4, other arithmetic, kernel_terms(): taps.append(jnp.sum(grad_f * window.astype(jnp.float32), axis=leading))  8.17 us
    reduce_sum x1, other arithmetic, block_step(): row_mean = jnp.mean(convolved, axis=-1, keepdims=True)  8.17 us
    another operation x7, local copies, waits for them, and re-layouts, kernel_terms(): stacked.append(jnp.stack(taps))  5.01 us
    unnamed x51, local copies, waits for them, and re-layouts  4.5 us
  transfers between devices with their start and end apart: 8, of which 2 were waited for; matrix products, arithmetic and copies ran while one was open for 9% of the time, Pallas kernels for 0%

profile of v1, /device:TPU:1, one launch (start us, length us, event | category | flops | bytes accessed | tf_op | source)
XLA Modules:
  0.0 157.6 jit_solution(8239802872290906471)
XLA Ops:
  3.2 8.8 %collective-permute-start.2 = (bf16[1,16,3,256]{3,2,1,0:T(4,128)(2,1)S(1)}, bf16[1,16,3,256]{3,2,1,0:T(4,128)(2,1)S(1)}, u32[]{:S(2)}, u32[]{:S(2)}) collective-permute-start(bf16[1,16,3,256]{3,2,1,0:T(4,128)(2,1)S(1)} %get-tuple-element.105), channel_id=1, source_target_pairs={{2,0},{4,2},{6,4},{8,6},{10,8},{12,10},{14,12},{16,14},{18,16},{20... | collective-permute-start | bytes 73736 | tf_op jit(solution)/shard_map/ppermute | solution.py:291
  12.0 1.9 %collective-permute-start.1 = (bf16[1,16,3,256]{3,2,1,0:T(4,128)(2,1)S(1)}, bf16[1,16,3,256]{3,2,1,0:T(4,128)(2,1)S(1)}, u32[]{:S(2)}, u32[]{:S(2)}) collective-permute-start(bf16[1,16,3,256]{3,2,1,0:T(4,128)(2,1)S(1)} %get-tuple-element.106), channel_id=1, source_target_pairs={{0,2},{2,4},{4,6},{6,8},{8,10},{10,12},{12,14},{14,16},{16,18},{18... | collective-permute-start | bytes 73736 | tf_op jit(solution)/shard_map/ppermute | solution.py:291
  14.0 1.9 %collective-permute-start = (bf16[2,1,16,3,256]{4,3,2,1,0:T(4,128)(2,1)S(1)}, bf16[2,1,16,3,256]{4,3,2,1,0:T(4,128)(2,1)S(1)}, u32[]{:S(2)}, u32[]{:S(2)}) collective-permute-start(bf16[2,1,16,3,256]{4,3,2,1,0:T(4,128)(2,1)S(1)} %pad_maximum_fusion.2), channel_id=1, source_target_pairs={{0,256},{256,0},{2,258},{258,2},{4,260},{260,4},{6,262},{262,6},{8... | collective-permute-start | bytes 147464 | tf_op jit(solution)/shard_map/ppermute | solution.py:301
  18.0 2.4 %collective-permute-done = bf16[2,1,16,3,256]{4,3,2,1,0:T(4,128)(2,1)S(1)} collective-permute-done((bf16[2,1,16,3,256]{4,3,2,1,0:T(4,128)(2,1)S(1)}, bf16[2,1,16,3,256]{4,3,2,1,0:T(4,128)(2,1)S(1)}, u32[]{:S(2)}, u32[]{:S(2)}) %collective-permute-start) | collective-permute-done | bytes 49184 | tf_op jit(solution)/shard_map/ppermute | solution.py:301
  21.0 5.5 %collective-permute-start.3 = (bf16[1,3,54,256]{3,2,1,0:T(8,128)(2,1)S(1)}, bf16[1,3,54,256]{3,2,1,0:T(8,128)(2,1)S(1)}, u32[]{:S(2)}, u32[]{:S(2)}) collective-permute-start(bf16[1,3,54,256]{3,2,1,0:T(8,128)(2,1)S(1)} %slice.905), channel_id=1, source_target_pairs={{0,256},{256,0},{2,258},{258,2},{4,260},{260,4},{6,262},{262,6},{8... | collective-permute-start | bytes 248840 | tf_op jit(solution)/shard_map/ppermute | solution.py:301
  29.3 8.2 %fusion.262 = (f32[16,48]{1,0:T(8,128)S(1)}, f32[1,16,48,256]{3,2,1,0:T(8,128)S(1)}) fusion(bf16[1,3,54,256]{3,2,1,0:T(8,128)(2,1)S(1)} %fusion.246, bf16[1,16,54,256]{3,2,1,0:T(8,128)(2,1)S(1)} %dynamic_update_slice.6, f32[256]{0:T(256)S(1)} %bitcast.387, f32[256]{0:T(256)S(1)} %bitcast.385, f32[256]{0:T(256)S(1)} %bitcast.383, f32[256]{0:T(256)S(1)} %bitcast.381, ...), kind=kLoop, calls=%fused_computation.498 | loop fusion | flops 41286912 | bytes 4136960 | tf_op jit(solution)/shard_map/reduce_sum | solution.py:358
  40.6 2.0 %fusion.221 = (f32[256]{0:T(256)}, bf16[768,256]{1,0:T(8,128)(2,1)}, bf16[768,256]{1,0:T(8,128)(2,1)S(1)}) fusion(f32[768]{0:T(1024)S(1)} %broadcast_in_dim.17, bf16[1,3,16,16,256]{4,3,2,1,0:T(8,128)(2,1)S(1)} %copy-done.9, f32[256]{0:T(256)S(1)} %copy-done.21, bf16[1,3,16,16,256]{4,3,1,2,0:T(8,128)(2,1)S(1)} %copy_multiply_fusion, ...), kind=kOutput, calls=%fused_computation.403 | convolution fusion | flops 405012224 | bytes 3675136 | tf_op jit(solution)/shard_map/dot_general | solution.py:366
  42.6 3.4 %fusion.13 = (bf16[1024,768]{0,1:T(8,128)(2,1)}, f32[768,1024]{1,0:T(8,128)S(1)}) fusion(f32[768,1024]{1,0:T(8,128)S(1)} %get-tuple-element.165, bf16[768,256]{1,0:T(8,128)(2,1)S(1)} %get-tuple-element.104, bf16[1024,256]{1,0:T(8,128)(2,1)S(1)} %copy-done), kind=kOutput, calls=%fused_computation.135 | convolution fusion | flops 418381824 | bytes 8781824 | tf_op jit(solution)/shard_map/dot_general | solution.py:376
  46.0 3.1 %multiply_reduce_fusion = (f32[256]{0:T(256)}, f32[768]{0:T(1024)S(1)}, f32[768]{0:T(1024)S(1)}, f32[768,256]{1,0:T(8,128)S(1)}) fusion(f32[1,16,48,256]{3,2,1,0:T(8,128)S(1)} %get-tuple-element.95, f32[768]{0:T(1024)S(1)} %rsqrt.13, f32[768]{0:T(1024)S(1)} %div.15, f32[256]{0:T(256)S(1)} %copy-done.14, bf16[256,1024]{1,0:T(8,128)(2,1)S(1)} %copy-done.20, ...), kind=kOutput, calls=%fused_computation.406 | convolution fusion | flops 419952896 | bytes 8402944 | tf_op jit(solution)/shard_map/dot_general | solution.py:384
  49.6 1.8 %fusion.213 = (f32[256]{0:T(256)}, f32[256]{0:T(256)}, f32[256]{0:T(256)}, f32[256]{0:T(256)}, f32[256]{0:T(256)}, /*index=5*/f32[256]{0:T(256)}, f32[256]{0:T(256)}, f32[256]{0:T(256)}, f32[256]{0:T(256)}) fusion(bf16[1,16,48,256]{3,2,1,0:T(8,128)(2,1)S(1)} %bitcast.269, bf16[1,3,54,256]{3,2,1,0:T(8,128)(2,1)S(1)} %fusion.246, ...), kind=kLoop, calls=%fused_computation.391 | loop fusion | flops 7272192 | bytes 927744 | tf_op jit(solution)/shard_map/reduce_sum | solution.py:329
  51.4 1.8 %fusion.214 = (f32[256]{0:T(256)}, f32[256]{0:T(256)}, f32[256]{0:T(256)}, f32[256]{0:T(256)}, f32[256]{0:T(256)}, /*index=5*/f32[256]{0:T(256)}, f32[256]{0:T(256)}, f32[256]{0:T(256)}, f32[256]{0:T(256)}) fusion(bf16[1,16,48,256]{3,2,1,0:T(8,128)(2,1)S(1)} %bitcast.270, bf16[1,3,54,256]{3,2,1,0:T(8,128)(2,1)S(1)} %fusion.246, ...), kind=kLoop, calls=%fused_computation.392 | loop fusion | flops 10811136 | bytes 927744 | tf_op jit(solution)/shard_map/reduce_sum | solution.py:329
  53.2 2.2 %fusion.212 = (f32[256]{0:T(256)}, f32[256]{0:T(256)}, f32[256]{0:T(256)}, f32[256]{0:T(256)}, f32[256]{0:T(256)}, /*index=5*/f32[256]{0:T(256)}, f32[256]{0:T(2...) fusion(bf16[1,16,48,256]{3,2,1,0:T(8,128)(2,1)S(1)} %bitcast.27, ...), kind=kLoop, calls=%fused_computation.390 | loop fusion | flops 9629952 | bytes 933888 | tf_op jit(solution)/shard_map/reduce_sum | solution.py:329
  55.4 2.3 %fusion.193 = (f32[256]{0:T(256)}, f32[256]{0:T(256)}, f32[256]{0:T(256)}, f32[256]{0:T(256)}, f32[256]{0:T(256)}, /*index=5*/f32[256]{0:T(256)}, f32[256]{0:T(2...) fusion(bf16[1,16,48,256]{3,2,1,0:T(8,128)(2,1)S(1)} %bitcast.27, ...), kind=kLoop, calls=%fused_computation.371 | loop fusion | flops 9629696 | bytes 3620864 | tf_op jit(solution)/shard_map/reduce_sum | solution.py:329
  57.8 10.0 %fusion.114 = f32[1,22,54,256]{3,2,1,0:T(8,128)S(1)} fusion(f32[1,16,48,256]{3,2,1,0:T(8,128)S(1)} %convert.16, f32[256]{0:T(256)S(1)} %bitcast.388, f32[256]{0:T(256)S(1)} %bitcast.386, f32[256]{0:T(256)S(1)} %bitcast.384, f32[256]{0:T(256)S(1)} %bitcast.382, f32[256]{0:T(256)S(1)} %bitcast.380, f32[256]{0:T(256)S(1)} %bitcast.378, f32[256]{0:T(256)S(1)} %bitcast.376, ...), kind=kLoop, calls=%fused_computation.239 | loop fusion | flops 29500416 | bytes 2053120 | tf_op jit(solution)/shard_map/add | solution.py:350
  68.6 2.0 %copy.40 = bf16[256,768]{1,0:T(8,128)(2,1)} copy(bf16[256,768]{0,1:T(8,128)(2,1)} %bitcast.287) | data formatting | bytes 786432 | tf_op jit(solution)/shard_map/dot_general | solution.py:373
  70.6 1.6 %fusion.17 = f32[1024,2,128]{2,0,1:T(8,128)S(1)} fusion(bf16[2,128,768]{2,1,0:T(8,128)(2,1)} %bitcast.282, bf16[768,1024]{1,0:T(8,128)(2,1)S(1)} %copy-done.5), kind=kOutput, calls=%fused_computation.143 | convolution fusion | flops 402653184 | bytes 3014656 | tf_op jit(solution)/shard_map/dot_general | solution.py:373
  72.3 1.8 %copy.38 = bf16[1024,768]{1,0:T(8,128)(2,1)S(1)} copy(bf16[1024,768]{0,1:T(8,128)(2,1)} %get-tuple-element.167) | data formatting | bytes 3145728 | tf_op jit(solution)/shard_map/dot_general | solution.py:381
  83.3 1.4 reshape.520
  86.6 41.4 %shard_map.144 = (bf16[2,2048,128]{2,1,0:T(8,128)(2,1)S(1)}, f32[2,64,128]{2,1,0:T(8,128)S(1)}) custom-call(f32[2,2048,128]{2,1,0:T(8,128)S(1)} %pad_maximum_fusion.wide, f32[2,64,128]{2,1,0:T(8,128)S(1)} %pad_maximum_fusion.4.small), custom_call_target="tpu_custom_call" | custom-call | tf_op jit(solution)/shard_map/pallas_call | solution.py:249
  128.8 3.6 %collective-permute-start.4 = (bf16[1,3,54,256]{3,2,1,0:T(8,128)(2,1)S(1)}, bf16[1,3,54,256]{3,2,1,0:T(8,128)(2,1)S(1)}, u32[]{:S(2)}, u32[]{:S(2)}) collective-permute-start(bf16[1,3,54,256]{3,2,1,0:T(8,128)(2,1)S(1)} %fusion.244), channel_id=1, source_target_pairs={{0,256},{256,0},{2,258},{258,2},{4,260},{260,4},{6,262},{262,6},{8... | collective-permute-start | bytes 248840 | tf_op jit(solution)/shard_map/ppermute | solution.py:301
  134.3 1.9 %collective-permute-done.4 = bf16[1,3,54,256]{3,2,1,0:T(8,128)(2,1)S(1)} collective-permute-done((bf16[1,3,54,256]{3,2,1,0:T(8,128)(2,1)S(1)}, bf16[1,3,54,256]{3,2,1,0:T(8,128)(2,1)S(1)}, u32[]{:S(2)}, u32[]{:S(2)}) %collective-permute-start.4) | collective-permute-done | bytes 82976 | tf_op jit(solution)/shard_map/ppermute | solution.py:301
  136.9 2.8 %collective-permute-start.7 = (bf16[1,16,3,256]{3,2,1,0:T(4,128)(2,1)}, bf16[1,16,3,256]{3,2,1,0:T(4,128)(2,1)}, u32[]{:S(2)}, u32[]{:S(2)}) collective-permute-start(bf16[1,16,3,256]{3,2,1,0:T(4,128)(2,1)} %get-tuple-element.100), channel_id=1, source_target_pairs={{2,0},{4,2},{6,4},{8,6},{10,8},{12,10},{14,12},{16,14},{18,16},{20... | collective-permute-start | bytes 73736 | tf_op jit(solution)/shard_map/ppermute | solution.py:291
  139.8 3.8 %collective-permute-start.6 = (bf16[1,16,3,256]{3,2,1,0:T(4,128)(2,1)}, bf16[1,16,3,256]{3,2,1,0:T(4,128)(2,1)}, u32[]{:S(2)}, u32[]{:S(2)}) collective-permute-start(bf16[1,16,3,256]{3,2,1,0:T(4,128)(2,1)} %get-tuple-element.101), channel_id=1, source_target_pairs={{0,2},{2,4},{4,6},{6,8},{8,10},{10,12},{12,14},{14,16},{16,18},{18... | collective-permute-start | bytes 73736 | tf_op jit(solution)/shard_map/ppermute | solution.py:291
  145.0 3.5 %collective-permute-start.5 = (bf16[2,1,16,3,256]{4,3,2,1,0:T(4,128)(2,1)}, bf16[2,1,16,3,256]{4,3,2,1,0:T(4,128)(2,1)}, u32[]{:S(2)}, u32[]{:S(2)}) collective-permute-start(bf16[2,1,16,3,256]{4,3,2,1,0:T(4,128)(2,1)} %pad_maximum_fusion.3), channel_id=1, source_target_pairs={{0,256},{256,0},{2,258},{258,2},{4,260},{260,4},{6,262},{262,6},{8... | collective-permute-start | bytes 147464 | tf_op jit(solution)/shard_map/ppermute | solution.py:301
  (125 shorter events, 36.4 us)
Async XLA Ops:
  0.6 39.9 %copy-start = (bf16[1024,256]{1,0:T(8,128)(2,1)S(1)}, bf16[1024,256]{1,0:T(8,128)(2,1)}, u32[]{:S(2)}) copy-start(bf16[1024,256]{1,0:T(8,128)(2,1)} %param.20) | copy-start | bytes 1572868
  3.2 14.9 %collective-permute-start.2 = (bf16[1,16,3,256]{3,2,1,0:T(4,128)(2,1)S(1)}, bf16[1,16,3,256]{3,2,1,0:T(4,128)(2,1)S(1)}, u32[]{:S(2)}, u32[]{:S(2)}) collective-permute-start(bf16[1,16,3,256]{3,2,1,0:T(4,128)(2,1)S(1)} %get-tuple-element.105), channel_id=1, source_target_pairs={{2,0},{4,2},{6,4},{8,6},{10,8},{12,10},{14,12},{16,14},{18,16},{20... | collective-permute-start | bytes 73736 | tf_op jit(solution)/shard_map/ppermute | solution.py:291
  12.0 6.1 %collective-permute-start.1 = (bf16[1,16,3,256]{3,2,1,0:T(4,128)(2,1)S(1)}, bf16[1,16,3,256]{3,2,1,0:T(4,128)(2,1)S(1)}, u32[]{:S(2)}, u32[]{:S(2)}) collective-permute-start(bf16[1,16,3,256]{3,2,1,0:T(4,128)(2,1)S(1)} %get-tuple-element.106), channel_id=1, source_target_pairs={{0,2},{2,4},{4,6},{6,8},{8,10},{10,12},{12,14},{14,16},{16,18},{18... | collective-permute-start | bytes 73736 | tf_op jit(solution)/shard_map/ppermute | solution.py:291
  14.0 6.5 %collective-permute-start = (bf16[2,1,16,3,256]{4,3,2,1,0:T(4,128)(2,1)S(1)}, bf16[2,1,16,3,256]{4,3,2,1,0:T(4,128)(2,1)S(1)}, u32[]{:S(2)}, u32[]{:S(2)}) collective-permute-start(bf16[2,1,16,3,256]{4,3,2,1,0:T(4,128)(2,1)S(1)} %pad_maximum_fusion.2), channel_id=1, source_target_pairs={{0,256},{256,0},{2,258},{258,2},{4,260},{260,4},{6,262},{262,6},{8... | collective-permute-start | bytes 147464 | tf_op jit(solution)/shard_map/ppermute | solution.py:301
  21.0 8.0 %collective-permute-start.3 = (bf16[1,3,54,256]{3,2,1,0:T(8,128)(2,1)S(1)}, bf16[1,3,54,256]{3,2,1,0:T(8,128)(2,1)S(1)}, u32[]{:S(2)}, u32[]{:S(2)}) collective-permute-start(bf16[1,3,54,256]{3,2,1,0:T(8,128)(2,1)S(1)} %slice.905), channel_id=1, source_target_pairs={{0,256},{256,0},{2,258},{258,2},{4,260},{260,4},{6,262},{262,6},{8... | collective-permute-start | bytes 248840 | tf_op jit(solution)/shard_map/ppermute | solution.py:301
  27.5 9.9 %copy-start.15 = (f32[1,1,256]{2,1,0:T(1,128)}, f32[1,1,256]{2,1,0:T(1,128)S(1)}, u32[]{:S(2)}) copy-start(f32[1,1,256]{2,1,0:T(1,128)S(1)} %get-tuple-element.163) | copy-start | bytes 3076
  29.3 8.7 %copy-start.14 = (f32[256]{0:T(256)S(1)}, f32[256]{0:T(256)}, u32[]{:S(2)}) copy-start(f32[256]{0:T(256)} %param.18) | copy-start | bytes 3076
  42.6 3.4 %copy-start.8 = (bf16[768,256]{1,0:T(8,128)(2,1)}, bf16[768,256]{1,0:T(8,128)(2,1)S(1)}, u32[]{:S(2)}) copy-start(bf16[768,256]{1,0:T(8,128)(2,1)S(1)} %get-tuple-element.104) | copy-start | bytes 1179652
  55.4 2.4 %copy-start.16 = (f32[1,1,256]{2,1,0:T(1,128)S(1)}, f32[1,1,256]{2,1,0:T(1,128)}, u32[]{:S(2)}) copy-start(f32[1,1,256]{2,1,0:T(1,128)} %copy-done.15) | copy-start | bytes 3076
  67.9 2.7 %copy-start.1 = (f32[1,22,54,256]{3,2,1,0:T(8,128)}, f32[1,22,54,256]{3,2,1,0:T(8,128)S(1)}, u32[]{:S(2)}) copy-start(f32[1,22,54,256]{3,2,1,0:T(8,128)S(1)} %fusion.114) | copy-start | bytes 3649540
  72.2 9.7 %copy-start.17 = (f32[256]{0:T(256)S(1)}, f32[256]{0:T(256)}, u32[]{:S(2)}) copy-start(f32[256]{0:T(256)} %get-tuple-element.53) | copy-start | bytes 3076
  72.2 9.7 %copy-start.18 = (f32[256]{0:T(256)S(1)}, f32[256]{0:T(256)}, u32[]{:S(2)}) copy-start(f32[256]{0:T(256)} %get-tuple-element.60) | copy-start | bytes 3076
  72.2 13.4 %copy-start.6 = (bf16[1,16,48,256]{3,2,1,0:T(8,128)(2,1)S(1)}, bf16[1,16,48,256]{3,2,1,0:T(8,128)(2,1)}, u32[]{:S(2)}) copy-start(bf16[1,16,48,256]{3,2,1,0:T(8,128)(2,1)} %multiply_convert_fusion.1) | copy-start | bytes 1179652
  86.5 42.0 %copy-start.11 = (bf16[1,3,54,256]{3,2,1,0:T(8,128)(2,1)S(1)}, bf16[1,3,54,256]{3,2,1,0:T(8,128)(2,1)}, u32[]{:S(2)}) copy-start(bf16[1,3,54,256]{3,2,1,0:T(8,128)(2,1)} %slice.968) | copy-start | bytes 248836
  128.8 7.4 %collective-permute-start.4 = (bf16[1,3,54,256]{3,2,1,0:T(8,128)(2,1)S(1)}, bf16[1,3,54,256]{3,2,1,0:T(8,128)(2,1)S(1)}, u32[]{:S(2)}, u32[]{:S(2)}) collective-permute-start(bf16[1,3,54,256]{3,2,1,0:T(8,128)(2,1)S(1)} %fusion.244), channel_id=1, source_target_pairs={{0,256},{256,0},{2,258},{258,2},{4,260},{260,4},{6,262},{262,6},{8... | collective-permute-start | bytes 248840 | tf_op jit(solution)/shard_map/ppermute | solution.py:301
  132.5 3.7 %copy-start.2 = (f32[1,22,54,256]{3,2,1,0:T(8,128)S(1)}, f32[1,22,54,256]{3,2,1,0:T(8,128)}, u32[]{:S(2)}) copy-start(f32[1,22,54,256]{3,2,1,0:T(8,128)} %copy-done.1) | copy-start | bytes 3649540
  132.5 3.7 %slice-start = ((f32[1,22,54,256]{3,2,1,0:T(8,128)}), f32[1,16,54,256]{3,2,1,0:T(8,128)S(1)}, s32[]{:S(2)}) async-start(f32[1,22,54,256]{3,2,1,0:T(8,128)} %copy-done.1), calls=%async_computation | async-start | bytes 1835008 | tf_op jit(solution)/shard_map/slice | solution.py:472
  132.5 16.5 %copy-start.7 = (bf16[768,256]{1,0:T(8,128)(2,1)S(1)}, bf16[768,256]{1,0:T(8,128)(2,1)}, u32[]{:S(2)}) copy-start(bf16[768,256]{1,0:T(8,128)(2,1)} %get-tuple-element.103) | copy-start | bytes 1179652
  133.7 17.6 %copy-start.3 = (f32[1,2048,128]{2,1,0:T(8,128)S(1)}, f32[1,2048,128]{2,1,0:T(8,128)}, u32[]{:S(2)}) copy-start(f32[1,2048,128]{2,1,0:T(8,128)} %get-tuple-element.98) | copy-start | bytes 3145732
  136.9 17.5 %collective-permute-start.7 = (bf16[1,16,3,256]{3,2,1,0:T(4,128)(2,1)}, bf16[1,16,3,256]{3,2,1,0:T(4,128)(2,1)}, u32[]{:S(2)}, u32[]{:S(2)}) collective-permute-start(bf16[1,16,3,256]{3,2,1,0:T(4,128)(2,1)} %get-tuple-element.100), channel_id=1, source_target_pairs={{2,0},{4,2},{6,4},{8,6},{10,8},{12,10},{14,12},{16,14},{18,16},{20... | collective-permute-start | bytes 73736 | tf_op jit(solution)/shard_map/ppermute | solution.py:291
  139.8 14.7 %collective-permute-start.6 = (bf16[1,16,3,256]{3,2,1,0:T(4,128)(2,1)}, bf16[1,16,3,256]{3,2,1,0:T(4,128)(2,1)}, u32[]{:S(2)}, u32[]{:S(2)}) collective-permute-start(bf16[1,16,3,256]{3,2,1,0:T(4,128)(2,1)} %get-tuple-element.101), channel_id=1, source_target_pairs={{0,2},{2,4},{4,6},{6,8},{8,10},{10,12},{12,14},{14,16},{16,18},{18... | collective-permute-start | bytes 73736 | tf_op jit(solution)/shard_map/ppermute | solution.py:291
  145.0 8.5 %collective-permute-start.5 = (bf16[2,1,16,3,256]{4,3,2,1,0:T(4,128)(2,1)}, bf16[2,1,16,3,256]{4,3,2,1,0:T(4,128)(2,1)}, u32[]{:S(2)}, u32[]{:S(2)}) collective-permute-start(bf16[2,1,16,3,256]{4,3,2,1,0:T(4,128)(2,1)} %pad_maximum_fusion.3), channel_id=1, source_target_pairs={{0,256},{256,0},{2,258},{258,2},{4,260},{260,4},{6,262},{262,6},{8... | collective-permute-start | bytes 147464 | tf_op jit(solution)/shard_map/ppermute | solution.py:301
  153.4 3.2 %copy-start.10 = (bf16[1,3,16,16,256]{4,3,2,1,0:T(8,128)(2,1)S(1)}, bf16[1,3,16,16,256]{4,3,2,1,0:T(8,128)(2,1)}, u32[]{:S(2)}) copy-start(bf16[1,3,16,16,256]{4,3,2,1,0:T(8,128)(2,1)} %param.14) | copy-start | bytes 1179652
  153.4 3.2 %copy-start.19 = (f32[48]{0:T(128)S(1)}, f32[48]{0:T(128)}, u32[]{:S(2)}) copy-start(f32[48]{0:T(128)} %broadcast_in_dim.38) | copy-start | bytes 580
  (7 other events, 10.4 us)

commit v2 on v0

v2 whole, which is shorter than its diff:
```python
import functools

import jax
import jax.numpy as jnp
from jax import lax
from jax.experimental import pallas as pl
from jax.experimental.pallas import tpu as pltpu
from jax.sharding import PartitionSpec as P

HID = 1024
KSIZE = 7
NX, NZ, NYH = 4, 8, 4
NY = 2 * NYH
GROUP_X, GROUP_Y, GROUP_Z = 1024, 512, 512
HALF = GROUP_X + GROUP_Y + GROUP_Z
Y0, Z0 = GROUP_X, GROUP_X + GROUP_Y
SMALL = 64
XR, YR, ZR = GROUP_X // NX, GROUP_Y // NY, GROUP_Z // NZ
XA, XB = XR // 2 // NY, XR // 2 // NZ
YX, ZX = YR // NX, ZR // NX
SR = SMALL // NY
F32, BF16 = jnp.float32, jnp.bfloat16


class Place:
    def __init__(self):
        t = lax.axis_index("tiles")
        self.t = t
        self.lo = lax.axis_index("dp")
        self.core = t % 2
        self.yh = (t // 2) % NYH
        self.z = (t // (2 * NYH)) % NZ
        self.x = t // (2 * NYH * NZ)
        self.y = self.yh * 2 + self.lo

    def along(self, axis, step):
        if axis == "core":
            place = 1 - self.core
            return place, (self.t + place - self.core, self.lo)
        if axis == "x":
            place = (self.x + step) % NX
            return place, (self.t + (place - self.x) * (2 * NYH * NZ), self.lo)
        if axis == "z":
            place = (self.z + step) % NZ
            return place, (self.t + (place - self.z) * (2 * NYH), self.lo)
        place = (self.y + step) % NY
        return place, (self.t + (place // 2 - self.yh) * 2, place % 2)


COUNT = {"x": NX, "y": NY, "z": NZ, "core": 2}


def steps(axis):
    n = COUNT[axis]
    near = []
    for d in range(1, n // 2 + 1):
        near += [d, n - d] if d != n - d else [d]
    return near


def send(src, dst, send_sem, recv_sem, device):
    pltpu.make_async_remote_copy(
        src_ref=src,
        dst_ref=dst,
        send_sem=send_sem,
        recv_sem=recv_sem,
        device_id=device,
        device_id_type=pl.DeviceIdType.MESH,
    ).start()


def await_bytes(like, sem):
    pltpu.make_async_copy(like, like, sem).wait()


def rows(start, size):
    return pl.ds(pl.multiple_of(start, size), size)


EPS = 1e-06
C = 256
TILE = 16
SLOTS = 3
CELLS = SLOTS * TILE * TILE
WIDE = 64
LEFT = 8
EDGE = KSIZE // 2
BAND = (TILE + 2 * EDGE) * WIDE
GELU_A = 0.7978845608028654
GELU_B = 0.044715


def halo_places(here):
    count = 2 * NX * NZ * NYH
    half = count // 2

    def swap(i):
        return i + (i // half) * (count + half - 1 - 2 * i)

    rank = swap(here.t)
    west = swap((rank + count - 1) % count)
    east = swap((rank + 1) % count)
    across = (here.t + half) % count
    across_west = (west + half) % count
    across_east = (east + half) % count
    return west, east, across, across_west, across_east


class Halo:
    def __init__(self, here, band, edges, top, got, got_top, ss, rs):
        self.here, self.band, self.edges, self.top = here, band, edges, top
        self.got, self.got_top, self.ss, self.rs = got, got_top, ss, rs
        self.west, self.east, self.across, self.across_west, self.across_east = halo_places(here)

    def gather_edges(self, owned):
        for h in range(2):
            lanes = pl.ds(h * 128, 128)
            for j in range(EDGE):
                start = EDGE * WIDE + LEFT + j
                left = self.band[h, pl.ds(start, TILE, WIDE), :]
                self.edges[0, j, :, lanes] = left.astype(BF16)
                ends = [
                    self.band[h, pl.ds(start + TILE * n - EDGE, TILE, WIDE), :]
                    for n in range(1, SLOTS + 1)
                ]
                right = jnp.where(owned == 1, ends[0], jnp.where(owned == 2, ends[1], ends[2]))
                self.edges[1, j, :, lanes] = right.astype(BF16)
            for k in range(EDGE):
                row = self.band[
                    h, pl.ds((TILE + k) * WIDE + LEFT, SLOTS * TILE), :
                ]
                self.top[k, :, lanes] = row.astype(BF16)

    def start(self):
        lo, ss, rs = self.here.lo, self.ss, self.rs
        left, right = self.edges.at[0], self.edges.at[1]
        send(left, self.got.at[1], ss.at[0], rs.at[1], (self.west, lo))
        send(right, self.got.at[0], ss.at[1], rs.at[0], (self.east, lo))
        send(self.top, self.got_top, ss.at[2], rs.at[2], (self.across, lo))
        for block, landing, i, device in (
            (left, self.got.at[2], 3, self.across_west),
            (right, self.got.at[3], 4, self.across_east),
        ):

            @pl.when(device != self.here.t)
            def _():
                send(block, landing, ss.at[i], rs.at[i], (device, lo))

            @pl.when(device == self.here.t)
            def _():
                pltpu.make_async_copy(block, landing, rs.at[i]).start()

    def finish(self, owned):
        edge = self.edges.at[0]
        await_bytes(edge, self.rs.at[0])
        await_bytes(edge, self.rs.at[1])
        for h in range(2):
            lanes = pl.ds(h * 128, 128)
            for j in range(EDGE):
                start = EDGE * WIDE + LEFT + j
                self.band[h, pl.ds(start - EDGE, TILE, WIDE), :] = self.got[0, j, :, lanes].astype(F32)
                east = self.got[1, j, :, lanes].astype(F32)
                for n in range(1, SLOTS):
                    spot = pl.ds(start + TILE * n, TILE, WIDE)
                    self.band[h, spot, :] = jnp.where(owned == n, east, self.band[h, spot, :])
                self.band[h, pl.ds(start + TILE * SLOTS, TILE, WIDE), :] = east
        await_bytes(self.top, self.rs.at[2])
        await_bytes(edge, self.rs.at[3])
        await_bytes(edge, self.rs.at[4])
        used = owned * TILE
        span = SLOTS * TILE
        spot = lax.broadcasted_iota(jnp.int32, (WIDE, 3 * span), 0) - LEFT
        item = lax.broadcasted_iota(jnp.int32, (WIDE, 3 * span), 1)
        inner = jnp.logical_and(jnp.logical_and(spot >= 0, spot < used), item == used - 1 - spot)
        for k in range(1, EDGE + 1):
            row = TILE - k
            west = jnp.logical_and(spot < 0, item == span + (-1 - spot) * TILE + row)
            west = jnp.logical_and(west, spot >= -EDGE)
            past = spot - used
            east = jnp.logical_and(past >= 0, item == 2 * span + (EDGE - 1 - past) * TILE + row)
            east = jnp.logical_and(east, past < EDGE)
            chosen = jnp.logical_or(inner, jnp.logical_or(west, east))
            pick = jnp.where(chosen, 1.0, 0.0).astype(BF16)
            source = jnp.concatenate(
                [
                    self.got_top[EDGE - k],
                    self.got[2].reshape(EDGE * TILE, C),
                    self.got[3].reshape(EDGE * TILE, C),
                ],
                axis=0,
            )
            fold = jnp.dot(pick, source, preferred_element_type=F32)
            place = pl.ds((EDGE + TILE - 1 + k) * WIDE, WIDE)
            self.band[0, place, :] = fold[:, :128]
            self.band[1, place, :] = fold[:, 128:]

    def drain(self):
        edge = self.edges.at[0]
        await_bytes(edge, self.ss.at[0])
        await_bytes(edge, self.ss.at[1])
        await_bytes(self.top, self.ss.at[2])
        for i, device in ((3, self.across_west), (4, self.across_east)):

            @pl.when(device != self.here.t)
            def _():
                await_bytes(edge, self.ss.at[i])


BLOCKS = SLOTS * TILE // 8


def block_start(block):
    return (block // 2) * (TILE * TILE) + (block % 2) * 8


def stencil(band, taps, h, block, backward):
    base = LEFT - EDGE + block * 8
    total = [None] * TILE
    for b in range(KSIZE):
        straight = [taps[h, pl.ds(a * KSIZE + b, 1), :] for a in range(KSIZE)]
        turned = straight
        if backward:
            turned = [
                taps[h, pl.ds((KSIZE - 1 - a) * KSIZE + KSIZE - 1 - b, 1), :] for a in range(KSIZE)
            ]
        for row in range(EDGE, TILE + 2 * EDGE):
            window = band[h, pl.ds(row * WIDE + base + b, 8), :]
            used = straight if row >= TILE + EDGE else turned
            for a in range(KSIZE):
                r = row - a
                if 0 <= r < TILE:
                    term = used[a] * window
                    total[r] = term if total[r] is None else total[r] + term
    return total


def total(first, landing):
    for k in range(landing.shape[0]):
        first = first + landing[k].astype(F32)
    return first


def line_total(landing):
    run = landing[0].astype(F32)
    for k in range(1, landing.shape[0]):
        run = run + landing[k].astype(F32)
    return run


class Reducer:
    def __init__(self, here, refs, ss, rs):
        self.here, self.ss, self.rs = here, ss, rs
        (
            self.wide, self.small, self.out, self.small_out, self.core_out, self.core_in, self.held, self.x_in,
            self.y_in, self.z_in, self.p_out, self.xa_in, self.xb_in, self.w_out, self.w_in, self.zz, self.yy,
            self.s_core, self.s_y, self.s_z, self.s_x, self.s_held,
        ) = refs
        self.partner = here.along("core", 1)[1]

    def gather(self, ref, axis, sem):
        for d in steps(axis):
            send(ref, ref, self.ss.at[sem], self.rs.at[sem], self.here.along(axis, d)[1])

    def scatter(self, ref, offset, size, landing, axis, sem):
        for d in steps(axis):
            place, device = self.here.along(axis, d)
            send(
                ref.at[rows(offset + place * size, size)], landing.at[d - 1], self.ss.at[sem], self.rs.at[sem], device
            )

    def core(self, k):
        span = rows(k * 512, 512)
        self.core_out[span] = self.wide[1 - self.here.core, span].astype(BF16)
        send(self.core_out.at[span], self.core_in.at[span], self.ss.at[k], self.rs.at[k], self.partner)

    def first_axis(self, region):
        axis, start, extent, size, landing, ks, sem = (
            ("x", 0, GROUP_X, XR, self.x_in, (0, 1), 4),
            ("y", Y0, GROUP_Y, YR, self.y_in, (2,), 5),
            ("z", Z0, GROUP_Z, ZR, self.z_in, (3,), 6),
        )[region]
        for k in ks:
            await_bytes(self.core_in.at[pl.ds(0, 512)], self.rs.at[k])
        span = pl.ds(start, extent)
        self.held[span] = (self.wide[self.here.core, span] + self.core_in[span].astype(F32)).astype(BF16)
        self.scatter(self.held, start, size, landing, axis, sem)

    def own(self, start, size):
        span = rows(start, size)
        return self.wide[self.here.core, span] + self.core_in[span].astype(F32)

    def second_axis(self):
        x, y, z = self.here.x, self.here.y, self.here.z
        await_bytes(self.x_in, self.rs.at[4])
        self.p_out[...] = total(self.own(x * XR, XR), self.x_in).astype(BF16)
        self.scatter(self.p_out, 0, XA, self.xa_in, "y", 8)
        self.scatter(self.p_out, XR // 2, XB, self.xb_in, "z", 9)
        await_bytes(self.y_in, self.rs.at[5])
        y_own = total(self.own(Y0 + y * YR, YR), self.y_in)
        for k in range(NX):
            self.w_out[k, :YX] = y_own[k * YX : (k + 1) * YX].astype(BF16)
        await_bytes(self.z_in, self.rs.at[6])
        z_own = total(self.own(Z0 + z * ZR, ZR), self.z_in)
        for k in range(NX):
            self.w_out[k, YX:] = z_own[k * ZX : (k + 1) * ZX].astype(BF16)
        for d in steps("x"):
            place, device = self.here.along("x", d)
            send(self.w_out.at[place], self.w_in.at[d - 1], self.ss.at[10], self.rs.at[10], device)

    def third_axis(self):
        x, y, z = self.here.x, self.here.y, self.here.z
        await_bytes(self.w_in, self.rs.at[10])
        mine = total(self.w_out[x].astype(F32), self.w_in)
        await_bytes(self.xa_in, self.rs.at[8])
        self.zz[z, :XA] = total(self.p_out[rows(y * XA, XA)].astype(F32), self.xa_in).astype(BF16)
        self.zz[z, XA:] = mine[:YX].astype(BF16)
        self.gather(self.zz.at[z], "z", 12)
        await_bytes(self.xb_in, self.rs.at[9])
        self.yy[y, :XB] = total(
            self.p_out[rows(XR // 2 + z * XB, XB)].astype(F32), self.xb_in
        ).astype(BF16)
        self.yy[y, XB:] = mine[YX:].astype(BF16)
        self.gather(self.yy.at[y], "y", 13)

    def second_back(self):
        c, x, y, z = self.here.core, self.here.x, self.here.y, self.here.z
        out = self.out
        await_bytes(self.zz.at[pl.ds(0, NZ - 1)], self.rs.at[12])
        zsum = line_total(self.zz).astype(BF16)
        out[c, rows(x * XR + y * XA, XA)] = zsum[:XA]
        out[c, rows(Y0 + y * YR + x * YX, YX)] = zsum[XA:]
        self.gather(out.at[c, rows(x * XR + y * XA, XA)], "y", 16)
        self.gather(out.at[c, rows(Y0 + y * YR + x * YX, YX)], "x", 17)
        await_bytes(self.yy.at[pl.ds(0, NY - 1)], self.rs.at[13])
        ysum = line_total(self.yy).astype(BF16)
        out[c, rows(x * XR + XR // 2 + z * XB, XB)] = ysum[:XB]
        out[c, rows(Z0 + z * ZR + x * ZX, ZX)] = ysum[XB:]
        self.gather(out.at[c, rows(x * XR + XR // 2 + z * XB, XB)], "z", 18)
        self.gather(out.at[c, rows(Z0 + z * ZR + x * ZX, ZX)], "x", 19)

    def bytes_of(self, count):
        return self.out.at[0, pl.ds(0, count)]

    def first_back(self):
        c, x, y, z = self.here.core, self.here.x, self.here.y, self.here.z
        await_bytes(self.bytes_of((NX - 1) * YX), self.rs.at[17])
        self.gather(self.out.at[c, rows(Y0 + y * YR, YR)], "y", 20)
        await_bytes(self.bytes_of((NX - 1) * ZX), self.rs.at[19])
        self.gather(self.out.at[c, rows(Z0 + z * ZR, ZR)], "z", 21)
        await_bytes(self.bytes_of((NY - 1) * XA), self.rs.at[16])
        await_bytes(self.bytes_of((NZ - 1) * XB), self.rs.at[18])
        self.gather(self.out.at[c, rows(x * XR, XR)], "x", 22)

    def core_back(self):
        c = self.here.core
        for sem, got, start, size, i in (
            (20, (NY - 1) * YR, Y0, GROUP_Y, 25),
            (21, (NZ - 1) * ZR, Z0, GROUP_Z, 26),
            (22, (NX - 1) * XR, 0, GROUP_X, 24),
        ):
            await_bytes(self.bytes_of(got), self.rs.at[sem])
            ref = self.out.at[c, pl.ds(start, size)]
            send(ref, ref, self.ss.at[i], self.rs.at[i], self.partner)

    def core_done(self):
        for i, size in ((25, GROUP_Y), (26, GROUP_Z), (24, GROUP_X)):
            await_bytes(self.bytes_of(size), self.rs.at[i])

    def small_core(self):
        send(self.small.at[1 - self.here.core], self.s_core, self.ss.at[27], self.rs.at[27], self.partner)

    def small_y(self):
        await_bytes(self.s_core, self.rs.at[27])
        self.s_held[...] = self.small[self.here.core] + self.s_core[...]
        self.scatter(self.s_held, 0, SR, self.s_y, "y", 7)

    def small_z(self):
        z = self.here.z
        await_bytes(self.s_y, self.rs.at[7])
        self.s_z[z] = total(self.s_held[rows(self.here.y * SR, SR)], self.s_y)
        self.gather(self.s_z.at[z], "z", 11)

    def small_x(self):
        x = self.here.x
        await_bytes(self.s_z.at[pl.ds(0, NZ - 1)], self.rs.at[11])
        self.s_x[x] = line_total(self.s_z)
        self.gather(self.s_x.at[x], "x", 14)

    def small_back(self):
        place = rows(self.here.y * SR, SR)
        await_bytes(self.s_x.at[pl.ds(0, NX - 1)], self.rs.at[14])
        self.small_out[self.here.core, place] = line_total(self.s_x)
        self.gather(self.small_out.at[self.here.core, place], "y", 15)

    def small_core_back(self):
        await_bytes(self.small_out.at[0, pl.ds(0, (NY - 1) * SR)], self.rs.at[15])
        ref = self.small_out.at[self.here.core]
        send(ref, ref, self.ss.at[23], self.rs.at[23], self.partner)

    def small_done(self):
        await_bytes(self.small_out.at[0], self.rs.at[23])

    def drain(self):
        ss = self.ss
        for k in range(4):
            await_bytes(self.core_out.at[pl.ds(0, 512)], ss.at[k])
        for ref, i in (
            (self.x_in, 4), (self.y_in, 5), (self.z_in, 6), (self.s_y, 7), (self.xa_in, 8), (self.xb_in, 9),
            (self.w_in, 10), (self.s_core, 27), (self.small_out.at[0], 23),
            (self.s_z.at[pl.ds(0, NZ - 1)], 11), (self.zz.at[pl.ds(0, NZ - 1)], 12),
            (self.yy.at[pl.ds(0, NY - 1)], 13), (self.s_x.at[pl.ds(0, NX - 1)], 14),
            (self.small_out.at[0, pl.ds(0, (NY - 1) * SR)], 15),
            (self.bytes_of((NY - 1) * XA), 16), (self.bytes_of((NX - 1) * YX), 17),
            (self.bytes_of((NZ - 1) * XB), 18), (self.bytes_of((NX - 1) * ZX), 19),
            (self.bytes_of((NY - 1) * YR), 20), (self.bytes_of((NZ - 1) * ZR), 21),
            (self.bytes_of((NX - 1) * XR), 22), (self.bytes_of(GROUP_X), 24), (self.bytes_of(GROUP_Y), 25),
            (self.bytes_of(GROUP_Z), 26),
        ):
            await_bytes(ref, ss.at[i])


def greet(here):
    barrier = pltpu.get_barrier_semaphore()
    mesh_id = pl.DeviceIdType.MESH
    greeted = 0
    for axis in ("core", "x", "y", "z"):
        for d in steps(axis):
            pl.semaphore_signal(barrier, inc=1, device_id=here.along(axis, d)[1], device_id_type=mesh_id)
            greeted += 1
    west, east, across, across_west, across_east = halo_places(here)
    for device in (west, east, across):
        pl.semaphore_signal(barrier, inc=1, device_id=(device, here.lo), device_id_type=mesh_id)
        greeted += 1
    for device in (across_west, across_east):

        @pl.when(device != here.t)
        def _():
            pl.semaphore_signal(barrier, inc=1, device_id=(device, here.lo), device_id_type=mesh_id)

    return barrier, greeted, (across_west, across_east)


def block_kernel(
    owned_ref, ocean_ref, fields, grad_out, kernel, ln_gain, w_in_hbm, w_out_hbm, layer_scale,
    state, grad_fields, wide_out, small_out,
    band, gband, taps, conv, inverse, normed, dproj, activated, dpreact, projected, dnormed, rowsum, weight_in,
    weight_out, edges, top, got, got_top, edges2, top2, got2, got_top2, small,
    wide, core_out, core_in, held, x_in, y_in, z_in, p_out, xa_in, xb_in, r_out, r_in, zz, yy,
    s_core, s_y, s_z, s_x, s_held, ss, rs, hs, hr, hs2, hr2, ls
):
    here = Place()
    barrier, greeted, maybe = greet(here)
    load_in = pltpu.make_async_copy(w_in_hbm, weight_in, ls.at[0])
    load_out = pltpu.make_async_copy(w_out_hbm, weight_out, ls.at[1])
    load_in.start()
    load_out.start()
    reducer = Reducer(
        here,
        (
            wide, small, wide_out, small_out, core_out, core_in, held, x_in, y_in, z_in, p_out, xa_in, xb_in,
            r_out, r_in, zz, yy, s_core, s_y, s_z, s_x, s_held,
        ),
        ss,
        rs,
    )
    owned = owned_ref[0]

    def slot_mask(slot):
        live = jnp.logical_and(slot < owned, ocean_ref[slot] > 0)
        return jnp.where(live, 1.0, 0.0).astype(F32)

    def clear(i, carry):
        spot = rows(i * 64, 64)
        for h in range(2):
            band[h, spot, :] = jnp.zeros((64, 128), F32)
            gband[h, spot, :] = jnp.zeros((64, 128), F32)
        return carry

    lax.fori_loop(0, BAND // 64, clear, 0)
    small[...] = jnp.zeros_like(small)
    rowsum[...] = jnp.zeros_like(rowsum)
    for a in range(KSIZE):
        line = kernel[a].astype(F32)
        for h in range(2):
            taps[h, a * KSIZE : (a + 1) * KSIZE, :] = line[:, h * 128 : (h + 1) * 128]

    def fill(i, carry):
        slot, r = i // TILE, i % TILE
        line = fields[rows(i * TILE, TILE), :].astype(F32) * slot_mask(slot)
        place = pl.ds(pl.multiple_of((EDGE + r) * WIDE + LEFT + slot * TILE, 8), TILE)
        band[0, place, :] = line[:, :128]
        band[1, place, :] = line[:, 128:]
        return carry

    lax.fori_loop(0, SLOTS * TILE, fill, 0)
    halo = Halo(here, band, edges, top, got, got_top, hs, hr)
    halo.gather_edges(owned)
    at_seam = jnp.logical_or(maybe[0] == here.t, maybe[1] == here.t)

    @pl.when(at_seam)
    def _():
        pl.semaphore_wait(barrier, greeted + 1)

    @pl.when(jnp.logical_not(at_seam))
    def _():
        pl.semaphore_wait(barrier, greeted + 2)

    halo.start()
    halo.finish(owned)

    def convolve(i, carry):
        h, block = i // BLOCKS, i % BLOCKS
        result = stencil(band, taps, h, block, False)
        for r in range(TILE):
            conv[h, pl.ds(pl.multiple_of(block_start(block) + r * TILE, 8), 8), :] = result[r]
        return carry

    lax.fori_loop(0, 2 * BLOCKS, convolve, 0)

    gain = [ln_gain[:, :128], ln_gain[:, 128:]]
    scale = [layer_scale[:, :128], layer_scale[:, 128:]]
    STEP = 64

    def norm(i, carry):
        span = rows(i * STEP, STEP)
        mask = slot_mask(i // (TILE * TILE // STEP))
        parts = [conv[h, span, :] for h in range(2)]
        mean = jnp.sum(parts[0] + parts[1], axis=1, keepdims=True) * (1.0 / C)
        centred = [part - mean for part in parts]
        variance = jnp.sum(
            centred[0] * centred[0] + centred[1] * centred[1], axis=1, keepdims=True
        ) * (1.0 / C)
        scaled = lax.rsqrt(variance + EPS)
        inverse[span, :] = jnp.broadcast_to(scaled, (STEP, 128))
        for h in range(2):
            lanes = pl.ds(h * 128, 128)
            yhat = centred[h] * scaled
            conv[h, span, :] = yhat
            normed[span, lanes] = (yhat * gain[h]).astype(BF16)
            cotangent = grad_out[span, lanes].astype(F32)
            dproj[span, lanes] = (mask * scale[h] * cotangent).astype(BF16)
        return carry

    lax.fori_loop(0, CELLS // STEP, norm, 0)
    load_in.wait()
    load_out.wait()
    across_rows = (((0,), (0,)), ((), ()))
    across_cols = (((1,), (1,)), ((), ()))

    def quarter(k, carry):
        part_in = weight_in[:, rows(k * 256, 256)]
        part_out = weight_out[rows(k * 256, 256), :]
        for m in range(SLOTS):
            span = pl.ds(m * 256, 256)
            cells, slopes = normed[span, :], dproj[span, :]
            v = jnp.dot(cells, part_in, preferred_element_type=F32)
            dact = lax.dot_general(slopes, part_out, across_cols, preferred_element_type=F32)
            square = v * v
            t = jnp.tanh(v * (GELU_A + (GELU_A * GELU_B) * square))
            half = 0.5 + 0.5 * t
            act = (v * half).astype(BF16)
            slope = half + (v * half) * (1.0 - t) * (GELU_A + (3.0 * GELU_A * GELU_B) * square)
            dpre = (dact * slope).astype(BF16)
            activated[span, :] = act
            dpreact[span, :] = dpre
            forward = jnp.dot(act, part_out, preferred_element_type=F32)
            back = lax.dot_general(dpre, part_in, across_cols, preferred_element_type=F32)
            first = k == 0
            projected[span, :] = jnp.where(first, forward, projected[span, :] + forward)
            dnormed[span, :] = jnp.where(first, back, dnormed[span, :] + back)
        grad_o = lax.dot_general(activated[...], dproj[...], across_rows, preferred_element_type=F32)
        grad_i = lax.dot_general(normed[...], dpreact[...], across_rows, preferred_element_type=F32)
        for h in range(2):
            spot = rows(k * 512 + h * 256, 256)
            wide[0, spot, :] = grad_i[:, h * 128 : (h + 1) * 128]
            wide[1, spot, :] = grad_o[:, h * 128 : (h + 1) * 128]
        reducer.core(k)
        return carry

    projected[...] = jnp.zeros_like(projected)
    dnormed[...] = jnp.zeros_like(dnormed)
    lax.fori_loop(0, HID // 256, quarter, 0)
    for region in range(3):
        reducer.first_axis(region)

    def norm_back(i, carry):
        span = rows(i * STEP, STEP)
        slot, r = i // (TILE * TILE // STEP), (i % (TILE * TILE // STEP)) * (STEP // TILE)
        lanes = [pl.ds(h * 128, 128) for h in range(2)]
        back = [dnormed[span, lanes[h]] for h in range(2)]
        yhat = [conv[h, span, :] for h in range(2)]
        for h in range(2):
            rowsum[h] += jnp.sum((back[h] * yhat[h]).reshape(STEP // 8, 8, 128), axis=0)
        dhat = [back[h] * gain[h] for h in range(2)]
        mean = jnp.sum(dhat[0] + dhat[1], axis=1, keepdims=True) * (1.0 / C)
        tilt = jnp.sum(dhat[0] * yhat[0] + dhat[1] * yhat[1], axis=1, keepdims=True) * (1.0 / C)
        for h in range(2):
            grad = inverse[span, :] * (dhat[h] - mean - yhat[h] * tilt)
            grad = grad.astype(BF16).astype(F32)
            for q in range(STEP // TILE):
                place = pl.ds(
                    pl.multiple_of((EDGE + r + q) * WIDE + LEFT + slot * TILE, 8), TILE
                )
                gband[h, place, :] = grad[q * TILE : (q + 1) * TILE]
        return carry

    lax.fori_loop(0, CELLS // STEP, norm_back, 0)
    halo_back = Halo(here, gband, edges2, top2, got2, got_top2, hs2, hr2)
    halo_back.gather_edges(owned)
    halo_back.start()

    def finish_state(i, carry):
        span = rows(i * STEP, STEP)
        mask = slot_mask(i // (TILE * TILE // STEP))
        for h in range(2):
            lanes = pl.ds(h * 128, 128)
            out = projected[span, lanes]
            rowsum[2 + h] += jnp.sum(
                (mask * grad_out[span, lanes].astype(F32) * out).reshape(STEP // 8, 8, 128), axis=0
            )
            kept = fields[span, lanes].astype(F32)
            state[span, lanes] = (mask * (kept + scale[h] * out)).astype(BF16)
        return carry

    lax.fori_loop(0, CELLS // STEP, finish_state, 0)
    reducer.second_axis()

    def kernel_grad(i, carry):
        h, b = i // KSIZE, i % KSIZE

        def one_block(block, sums):
            sums = list(sums)
            base = LEFT + block * 8
            cots = [gband[h, pl.ds(pl.multiple_of((EDGE + r) * WIDE + base, 8), 8), :] for r in range(TILE)]
            for row in range(EDGE, TILE + 2 * EDGE):
                window = band[h, pl.ds(row * WIDE + base - EDGE + b, 8), :]
                for a in range(KSIZE):
                    if 0 <= row - a < TILE:
                        sums[a] = sums[a] + cots[row - a] * window
            return tuple(sums)

        zero = tuple(jnp.zeros((8, 128), F32) for a in range(KSIZE))
        sums = lax.fori_loop(0, BLOCKS, one_block, zero)
        for a in range(KSIZE):
            small[h, pl.ds(a * KSIZE + b, 1), :] = jnp.sum(sums[a], axis=0, keepdims=True)
        return carry

    lax.fori_loop(0, 2 * KSIZE, kernel_grad, 0)
    for h in range(2):
        small[h, KSIZE * KSIZE : KSIZE * KSIZE + 1, :] = jnp.sum(rowsum[h], axis=0, keepdims=True)
        small[h, KSIZE * KSIZE + 1 : KSIZE * KSIZE + 2, :] = jnp.sum(rowsum[2 + h], axis=0, keepdims=True)
    reducer.small_core()
    reducer.third_axis()
    halo_back.finish(owned)
    reducer.small_y()

    def convolve_back(i, carry):
        h, block = i % 2, i // 2
        result = stencil(gband, taps, h, block, True)
        for r in range(TILE):
            conv[h, pl.ds(pl.multiple_of(block_start(block) + r * TILE, 8), 8), :] = result[r]
        return carry

    def finish_grad(i, carry):
        span = rows(i * STEP, STEP)
        mask = slot_mask(i // (TILE * TILE // STEP))
        for h in range(2):
            lanes = pl.ds(h * 128, 128)
            grad = mask * (grad_out[span, lanes].astype(F32) + conv[h, span, :])
            grad_fields[span, lanes] = grad.astype(BF16)
        return carry

    lax.fori_loop(0, BLOCKS, convolve_back, 0)
    reducer.second_back()
    reducer.small_z()
    lax.fori_loop(BLOCKS, 2 * BLOCKS, convolve_back, 0)
    reducer.first_back()
    reducer.small_x()
    lax.fori_loop(0, CELLS // STEP, finish_grad, 0)
    reducer.small_back()
    reducer.core_back()
    reducer.small_core_back()
    reducer.core_done()
    reducer.small_done()
    reducer.drain()
    halo.drain()
    halo_back.drain()


def block_call(block_count, ocean, fields, grad_out, kernel, ln_gain, w_in, w_out, layer_scale):
    vmem = pl.BlockSpec(memory_space=pltpu.VMEM)
    smem = pl.BlockSpec(memory_space=pltpu.SMEM)
    hbm = pl.BlockSpec(memory_space=pl.ANY)
    edges = pltpu.VMEM((2, EDGE, TILE, C), BF16)
    top = pltpu.VMEM((EDGE, SLOTS * TILE, C), BF16)
    got = pltpu.VMEM((4, EDGE, TILE, C), BF16)
    scratch = [
        pltpu.VMEM((2, BAND, 128), F32),
        pltpu.VMEM((2, BAND, 128), F32),
        pltpu.VMEM((2, 56, 128), F32),
        pltpu.VMEM((2, CELLS, 128), F32),
        pltpu.VMEM((CELLS, 128), F32),
        pltpu.VMEM((CELLS, C), BF16),
        pltpu.VMEM((CELLS, C), BF16),
        pltpu.VMEM((CELLS, 256), BF16),
        pltpu.VMEM((CELLS, 256), BF16),
        pltpu.VMEM((CELLS, C), F32),
        pltpu.VMEM((CELLS, C), F32),
        pltpu.VMEM((4, 8, 128), F32),
        pltpu.VMEM((C, HID), BF16),
        pltpu.VMEM((HID, C), BF16),
        edges, top, got, top, edges, top, got, top,
        pltpu.VMEM((2, SMALL, 128), F32),
        pltpu.VMEM((2, HALF, 128), F32),
        pltpu.VMEM((HALF, 128), BF16),
        pltpu.VMEM((HALF, 128), BF16),
        pltpu.VMEM((HALF, 128), BF16),
        pltpu.VMEM((NX - 1, XR, 128), BF16),
        pltpu.VMEM((NY - 1, YR, 128), BF16),
        pltpu.VMEM((NZ - 1, ZR, 128), BF16),
        pltpu.VMEM((XR, 128), BF16),
        pltpu.VMEM((NY - 1, XA, 128), BF16),
        pltpu.VMEM((NZ - 1, XB, 128), BF16),
        pltpu.VMEM((NX, YX + ZX, 128), BF16),
        pltpu.VMEM((NX - 1, YX + ZX, 128), BF16),
        pltpu.VMEM((NZ, XA + YX, 128), BF16),
        pltpu.VMEM((NY, XB + ZX, 128), BF16),
        pltpu.VMEM((SMALL, 128), F32),
        pltpu.VMEM((NY - 1, SR, 128), F32),
        pltpu.VMEM((NZ, SR, 128), F32),
        pltpu.VMEM((NX, SR, 128), F32),
        pltpu.VMEM((SMALL, 128), F32),
        pltpu.SemaphoreType.DMA((28,)),
        pltpu.SemaphoreType.DMA((28,)),
        pltpu.SemaphoreType.DMA((5,)),
        pltpu.SemaphoreType.DMA((5,)),
        pltpu.SemaphoreType.DMA((5,)),
        pltpu.SemaphoreType.DMA((5,)),
        pltpu.SemaphoreType.DMA((2,)),
    ]
    return pl.pallas_call(
        block_kernel,
        out_shape=(
            jax.ShapeDtypeStruct((CELLS, C), BF16),
            jax.ShapeDtypeStruct((CELLS, C), BF16),
            jax.ShapeDtypeStruct((2, HALF, 128), BF16),
            jax.ShapeDtypeStruct((2, SMALL, 128), F32),
        ),
        in_specs=[smem, smem, vmem, vmem, vmem, vmem, hbm, hbm, vmem],
        out_specs=(vmem, vmem, vmem, vmem),
        scratch_shapes=scratch,
        compiler_params=pltpu.CompilerParams(
            collective_id=1, has_side_effects=True, vmem_limit_bytes=48 * 1024 * 1024
        ),
    )(block_count, ocean, fields, grad_out, kernel, ln_gain, w_in, w_out, layer_scale)


def shards(fields, grad_out, block_count, ocean, kernel, ln_gain, w_in, w_out, layer_scale):
    shape = fields.shape
    samples, slot_count, tile_rows, tile_cols, channels = shape
    state, grad_fields, wide, small = block_call(
        block_count,
        ocean,
        fields.reshape(CELLS, channels),
        grad_out.reshape(CELLS, channels),
        kernel,
        ln_gain.reshape(1, channels),
        w_in,
        w_out,
        layer_scale.reshape(1, channels),
    )
    norm = (
        samples * lax.axis_size("dp") * slot_count * lax.axis_size("tiles") * tile_rows * tile_cols
    ) ** (-0.5)
    taps = KSIZE * KSIZE
    w_in_sum = jnp.transpose(wide[0].reshape(-1, channels, 128), (1, 0, 2)).reshape(channels, HID)
    w_out_sum = jnp.transpose(wide[1].reshape(4, 2, 256, 128), (0, 2, 1, 3)).reshape(HID, channels)
    small = jnp.concatenate([small[0], small[1]], axis=1) * norm
    return (
        state.reshape(shape),
        grad_fields.reshape(shape),
        small[:taps].reshape(KSIZE, KSIZE, channels),
        small[taps],
        w_in_sum.astype(F32) * norm,
        w_out_sum.astype(F32) * norm,
        small[taps + 1],
    )


def solution(mesh):
    placed = (
        P("dp", "tiles", None, None, None),
        P("dp", "tiles", None, None, None),
        P("tiles"),
        P("tiles"),
        P(),
        P(),
        P(),
        P(),
        P(),
    )
    return jax.shard_map(
        shards,
        mesh=mesh,
        in_specs=placed,
        out_specs=(
            P("dp", "tiles", None, None, None),
            P("dp", "tiles", None, None, None),
            P(),
            P(),
            P(),
            P(),
            P(),
        ),
        check_vma=False,
    )
```

time: 467 us -> 77.6 us (0.17)
  waiting for transfers between devices: 268 us -> 0 us
  blocking collectives: 104 us -> 0 us
  Pallas kernels: 0 us -> 64.5 us
  other arithmetic: 33.2 us -> 0.17 us
  starting transfers between devices: 27.6 us -> 0 us
  between operations: 15.9 us -> 1.35 us
  matrix products: 10.9 us -> 0 us
    psum x1 -> x0, waiting for transfers between devices: 256 us -> none  [shards(): lax.psum((kernel_part, gain_part, w_in_part, w_out_part, scale_part), ('t...]
    psum x1 -> x0, blocking collectives: 104 us -> none  [shards(): lax.psum((kernel_part, gain_part, w_in_part, w_out_part, scale_part), ('t...]
    pallas_call x0 -> x1, Pallas kernels: none -> 64.5 us  [block_call(): pl.pallas_call(block_kernel, out_shape=(jax.ShapeDtypeStruct((CELLS, C),...]
    ppermute x8 -> x0, starting transfers between devices: 27.6 us -> none  [the longest x4 18 us: passed_along(): return lax.ppermute(block, axis, route)]
    reduce_sum x6 -> x0, other arithmetic: 14.2 us -> none  [the longest x1 8.17 us: block_step(): row_mean = jnp.mean(convolved, axis=-1, keepdims=True)]
    ppermute x8 -> x0, waiting for transfers between devices: 11.6 us -> none  [the longest x4 11.6 us: from_partner(): return lax.ppermute(block, axis, route)]
    dot_general x6 -> x0, matrix products: 10.9 us -> none  [the longest x1 2.44 us: block_step(): lax.dot_general(dproj, w_out, (((1,), (1,)), ((), ())), preferred_element...]
    add x3 -> x0, other arithmetic: 10.1 us -> none  [the longest x1 10 us: spread(): running = running + kernel_f[row_shift, col_shift] * window]
  transfers between devices with their start and end apart: 9 -> 0, of which waited for: 5 -> 0; matrix products, arithmetic and copies ran while one was open for 2% -> 0% of each run, Pallas kernels for 0% -> 0%
where the time goes in v2:
time: 77.6 us; the launch traced here: 77.2 us
  Pallas kernels  64.5 us (83%)
  local copies, waits for them, and re-layouts  11.1 us (14%)
  between operations  1.35 us (2%)
    pallas_call x1, Pallas kernels, block_call(): pl.pallas_call(block_kernel, out_shape=(jax.ShapeDtypeStruct((CELLS, C),...  64.5 us
    unnamed x19, local copies, waits for them, and re-layouts  8.02 us

profile of v2, /device:TPU:1, one launch (start us, length us, event | category | flops | bytes accessed | tf_op | source)
XLA Modules:
  0.0 77.2 jit_solution(1565712582698659624)
XLA Ops:
  1.3 0.0 copy-start.6
  1.3 0.0 copy-start.5
  1.3 0.0 copy-start.7
  1.3 0.7 copy-done.6
  2.0 0.0 copy-done.5
  2.0 0.0 copy-done.7
  2.0 1.0 %copy-done = bf16[256,1024]{1,0:T(8,128)(2,1)S(1)} copy-done((bf16[256,1024]{1,0:T(8,128)(2,1)S(1)}, bf16[256,1024]{1,0:T(8,128)(2,1)}, u32[]{:S(2)}) %copy-start) | copy-done | bytes 524312
  3.0 0.0 copy-start.1
  3.0 1.0 %copy-done.1 = bf16[1024,256]{1,0:T(8,128)(2,1)S(1)} copy-done((bf16[1024,256]{1,0:T(8,128)(2,1)S(1)}, bf16[1024,256]{1,0:T(8,128)(2,1)}, u32[]{:S(2)}) %copy-start.1) | copy-done | bytes 524312
  4.1 0.0 copy-start.2
  4.1 1.0 %copy-done.2 = bf16[1,3,16,16,256]{4,3,2,1,0:T(8,128)(2,1)S(1)} copy-done((bf16[1,3,16,16,256]{4,3,2,1,0:T(8,128)(2,1)S(1)}, bf16[1,3,16,16,256]{4,3,2,1,0:T(8,128)(2,1)}, u32[]{:S(2)}) %copy-start.2) | copy-done | bytes 393240
  5.1 0.0 copy-start.3
  5.1 1.0 %copy-done.3 = bf16[1,3,16,16,256]{4,3,2,1,0:T(8,128)(2,1)S(1)} copy-done((bf16[1,3,16,16,256]{4,3,2,1,0:T(8,128)(2,1)S(1)}, bf16[1,3,16,16,256]{4,3,2,1,0:T(8,128)(2,1)}, u32[]{:S(2)}) %copy-start.3) | copy-done | bytes 393240
  6.1 0.0 copy-start.4
  6.1 0.7 copy-done.4
  6.8 64.5 %shard_map.144 = (bf16[768,256]{1,0:T(8,128)(2,1)S(1)}, bf16[768,256]{1,0:T(8,128)(2,1)S(1)}, bf16[2,2048,128]{2,1,0:T(8,128)(2,1)S(1)}, f32[2,64,128]{2,1,0:T(8,128)S(1)}) custom-call(s32[1]{0:T(128)S(6)} %copy.26.owned_ref, s32[3]{0:T(128)S(1)} %copy-done.7, bf16[768,256]{1,0:T(8,128)(2,1)S(1)} %bitcast.29, bf16[768,256]{1,0:T(8,128)(2,1)S(1)} %bitcast.30, ...), custom_call_target="tpu_custom_call" | custom-call | tf_op jit(solution)/shard_map/pallas_call | solution.py:741
  71.4 0.6 fusion
  72.0 0.6 reshape.55
  72.6 0.2 convert_multiply_fusion
  72.8 0.8 %copy.17 = f32[4,256,2,128]{3,2,1,0:T(2,128)S(1)} copy(f32[4,256,2,128]{3,1,2,0:T(8,128)S(1)} %bitcast.34) | data formatting | bytes 2097152 | tf_op jit(solution)/shard_map/mul | solution.py:785
  73.6 1.0 %copy.22 = f32[128,8,2,128]{3,1,2,0:T(8,128)} copy(f32[128,8,2,128]{3,2,1,0:T(2,128)S(1)} %bitcast.35) | data formatting | bytes 2097152
  74.6 1.1 %copy.23 = f32[8,32,8,128]{3,2,0,1:T(8,128)} copy(f32[8,32,8,128]{3,2,1,0:T(8,128)S(1)} %bitcast.33) | data formatting | bytes 2097152 | tf_op jit(solution)/shard_map/mul | solution.py:784
  75.7 0.7 copy.27
  76.5 0.7 copy.28
  (4 shorter events, 0.0 us)
Async XLA Ops:
  1.3 0.7 copy-start.6
  1.3 0.7 copy-start.5
  1.3 0.7 copy-start.7
  2.0 1.0 %copy-start = (bf16[256,1024]{1,0:T(8,128)(2,1)S(1)}, bf16[256,1024]{1,0:T(8,128)(2,1)}, u32[]{:S(2)}) copy-start(bf16[256,1024]{1,0:T(8,128)(2,1)} %w_in_hbm.1) | copy-start | bytes 1572868
  3.0 1.0 %copy-start.1 = (bf16[1024,256]{1,0:T(8,128)(2,1)S(1)}, bf16[1024,256]{1,0:T(8,128)(2,1)}, u32[]{:S(2)}) copy-start(bf16[1024,256]{1,0:T(8,128)(2,1)} %w_out_hbm.1) | copy-start | bytes 1572868
  4.1 1.0 %copy-start.2 = (bf16[1,3,16,16,256]{4,3,2,1,0:T(8,128)(2,1)S(1)}, bf16[1,3,16,16,256]{4,3,2,1,0:T(8,128)(2,1)}, u32[]{:S(2)}) copy-start(bf16[1,3,16,16,256]{4,3,2,1,0:T(8,128)(2,1)} %param.9) | copy-start | bytes 1179652
  5.1 1.0 %copy-start.3 = (bf16[1,3,16,16,256]{4,3,2,1,0:T(8,128)(2,1)S(1)}, bf16[1,3,16,16,256]{4,3,2,1,0:T(8,128)(2,1)}, u32[]{:S(2)}) copy-start(bf16[1,3,16,16,256]{4,3,2,1,0:T(8,128)(2,1)} %param.10) | copy-start | bytes 1179652
  6.1 0.7 copy-start.4

commit v3 on v2

--- a/solution.py
+++ b/solution.py
@@ -11,13 +11,10 @@
 KSIZE = 7
 NX, NZ, NYH = 4, 8, 4
 NY = 2 * NYH
-GROUP_X, GROUP_Y, GROUP_Z = 1024, 512, 512
-HALF = GROUP_X + GROUP_Y + GROUP_Z
-Y0, Z0 = GROUP_X, GROUP_X + GROUP_Y
+HALF = 2048
+REGION = HALF // 2
 SMALL = 64
-XR, YR, ZR = GROUP_X // NX, GROUP_Y // NY, GROUP_Z // NZ
-XA, XB = XR // 2 // NY, XR // 2 // NZ
-YX, ZX = YR // NX, ZR // NX
+PR, QR = REGION // (NX * NY), REGION // (NX * NZ)
 SR = SMALL // NY
 F32, BF16 = jnp.float32, jnp.bfloat16
 
@@ -32,6 +29,9 @@
         self.z = (t // (2 * NYH)) % NZ
         self.x = t // (2 * NYH * NZ)
         self.y = self.yh * 2 + self.lo
+
+    def device(self, core, x, y, z):
+        return (((x * NZ + z) * NYH + y // 2) * 2 + core, y % 2)
 
     def along(self, axis, step):
         if axis == "core":
@@ -56,6 +56,14 @@
     for d in range(1, n // 2 + 1):
         near += [d, n - d] if d != n - d else [d]
     return near
+
+
+def offsets(*sizes):
+    found = [()]
+    for n in sizes:
+        found = [step + (d,) for step in found for d in range(n)]
+    far = lambda step: -sum(min(d, n - d) for d, n in zip(step, sizes))
+    return sorted((step for step in found if any(step)), key=far)
 
 
 def send(src, dst, send_sem, recv_sem, device):
@@ -251,214 +259,174 @@
     def __init__(self, here, refs, ss, rs):
         self.here, self.ss, self.rs = here, ss, rs
         (
-            self.wide, self.small, self.out, self.small_out, self.core_out, self.core_in, self.held, self.x_in,
-            self.y_in, self.z_in, self.p_out, self.xa_in, self.xb_in, self.w_out, self.w_in, self.zz, self.yy,
-            self.s_core, self.s_y, self.s_z, self.s_x, self.s_held,
+            self.wide, self.small, self.out, self.small_out, self.core_out, self.core_in, self.held, self.p_in,
+            self.q_in, self.zz, self.yy, self.s_in, self.s_sum,
         ) = refs
-        self.partner = here.along("core", 1)[1]
-
-    def gather(self, ref, axis, sem):
-        for d in steps(axis):
-            send(ref, ref, self.ss.at[sem], self.rs.at[sem], self.here.along(axis, d)[1])
-
-    def scatter(self, ref, offset, size, landing, axis, sem):
-        for d in steps(axis):
-            place, device = self.here.along(axis, d)
-            send(
-                ref.at[rows(offset + place * size, size)], landing.at[d - 1], self.ss.at[sem], self.rs.at[sem], device
-            )
+        c, x, y, z = here.core, here.x, here.y, here.z
+        self.partner = here.device(1 - c, x, y, z)
+        self.regions = (
+            (0, PR, x * NY + y, self.p_in, self.zz, z, "z"),
+            (REGION, QR, x * NZ + z, self.q_in, self.yy, y, "y"),
+        )
+
+    def plane(self, region):
+        c, x, y, z = self.here.core, self.here.x, self.here.y, self.here.z
+        n = NZ if region else NY
+        for dx, d in offsets(NX, n):
+            px = (x + dx) % NX
+            if region:
+                pz = (z + d) % NZ
+                yield self.here.device(c, px, y, pz), px * NZ + pz, dx * n + d - 1
+            else:
+                py = (y + d) % NY
+                yield self.here.device(c, px, py, z), px * NY + py, dx * n + d - 1
 
     def core(self, k):
         span = rows(k * 512, 512)
         self.core_out[span] = self.wide[1 - self.here.core, span].astype(BF16)
         send(self.core_out.at[span], self.core_in.at[span], self.ss.at[k], self.rs.at[k], self.partner)
 
-    def first_axis(self, region):
-        axis, start, extent, size, landing, ks, sem = (
-            ("x", 0, GROUP_X, XR, self.x_in, (0, 1), 4),
-            ("y", Y0, GROUP_Y, YR, self.y_in, (2,), 5),
-            ("z", Z0, GROUP_Z, ZR, self.z_in, (3,), 6),
-        )[region]
-        for k in ks:
+    def scatter(self, region):
+        start, size, mine, landing, line, spot, axis = self.regions[region]
+        sem = 4 + region
+        for k in (2 * region, 2 * region + 1):
             await_bytes(self.core_in.at[pl.ds(0, 512)], self.rs.at[k])
-        span = pl.ds(start, extent)
+        span = pl.ds(start, REGION)
         self.held[span] = (self.wide[self.here.core, span] + self.core_in[span].astype(F32)).astype(BF16)
-        self.scatter(self.held, start, size, landing, axis, sem)
-
-    def own(self, start, size):
-        span = rows(start, size)
-        return self.wide[self.here.core, span] + self.core_in[span].astype(F32)
-
-    def second_axis(self):
-        x, y, z = self.here.x, self.here.y, self.here.z
-        await_bytes(self.x_in, self.rs.at[4])
-        self.p_out[...] = total(self.own(x * XR, XR), self.x_in).astype(BF16)
-        self.scatter(self.p_out, 0, XA, self.xa_in, "y", 8)
-        self.scatter(self.p_out, XR // 2, XB, self.xb_in, "z", 9)
-        await_bytes(self.y_in, self.rs.at[5])
-        y_own = total(self.own(Y0 + y * YR, YR), self.y_in)
-        for k in range(NX):
-            self.w_out[k, :YX] = y_own[k * YX : (k + 1) * YX].astype(BF16)
-        await_bytes(self.z_in, self.rs.at[6])
-        z_own = total(self.own(Z0 + z * ZR, ZR), self.z_in)
-        for k in range(NX):
-            self.w_out[k, YX:] = z_own[k * ZX : (k + 1) * ZX].astype(BF16)
-        for d in steps("x"):
-            place, device = self.here.along("x", d)
-            send(self.w_out.at[place], self.w_in.at[d - 1], self.ss.at[10], self.rs.at[10], device)
-
-    def third_axis(self):
-        x, y, z = self.here.x, self.here.y, self.here.z
-        await_bytes(self.w_in, self.rs.at[10])
-        mine = total(self.w_out[x].astype(F32), self.w_in)
-        await_bytes(self.xa_in, self.rs.at[8])
-        self.zz[z, :XA] = total(self.p_out[rows(y * XA, XA)].astype(F32), self.xa_in).astype(BF16)
-        self.zz[z, XA:] = mine[:YX].astype(BF16)
-        self.gather(self.zz.at[z], "z", 12)
-        await_bytes(self.xb_in, self.rs.at[9])
-        self.yy[y, :XB] = total(
-            self.p_out[rows(XR // 2 + z * XB, XB)].astype(F32), self.xb_in
-        ).astype(BF16)
-        self.yy[y, XB:] = mine[YX:].astype(BF16)
-        self.gather(self.yy.at[y], "y", 13)
-
-    def second_back(self):
-        c, x, y, z = self.here.core, self.here.x, self.here.y, self.here.z
-        out = self.out
-        await_bytes(self.zz.at[pl.ds(0, NZ - 1)], self.rs.at[12])
-        zsum = line_total(self.zz).astype(BF16)
-        out[c, rows(x * XR + y * XA, XA)] = zsum[:XA]
-        out[c, rows(Y0 + y * YR + x * YX, YX)] = zsum[XA:]
-        self.gather(out.at[c, rows(x * XR + y * XA, XA)], "y", 16)
-        self.gather(out.at[c, rows(Y0 + y * YR + x * YX, YX)], "x", 17)
-        await_bytes(self.yy.at[pl.ds(0, NY - 1)], self.rs.at[13])
-        ysum = line_total(self.yy).astype(BF16)
-        out[c, rows(x * XR + XR // 2 + z * XB, XB)] = ysum[:XB]
-        out[c, rows(Z0 + z * ZR + x * ZX, ZX)] = ysum[XB:]
-        self.gather(out.at[c, rows(x * XR + XR // 2 + z * XB, XB)], "z", 18)
-        self.gather(out.at[c, rows(Z0 + z * ZR + x * ZX, ZX)], "x", 19)
+        for device, place, slot in self.plane(region):
+            send(
+                self.held.at[rows(start + place * size, size)], landing.at[slot], self.ss.at[sem], self.rs.at[sem],
+                device,
+            )
+
+    def line(self, region):
+        start, size, mine, landing, line, spot, axis = self.regions[region]
+        sem = 6 + region
+        await_bytes(landing, self.rs.at[4 + region])
+        span = rows(start + mine * size, size)
+        own = self.wide[self.here.core, span] + self.core_in[span].astype(F32)
+        line[spot] = total(own, landing).astype(BF16)
+        for d in steps(axis)[::-1]:
+            send(line.at[spot], line.at[spot], self.ss.at[sem], self.rs.at[sem], self.here.along(axis, d)[1])
+
+    def gather(self, region):
+        start, size, mine, landing, line, spot, axis = self.regions[region]
+        sem = 8 + region
+        await_bytes(line.at[pl.ds(0, line.shape[0] - 1)], self.rs.at[6 + region])
+        span = rows(start + mine * size, size)
+        self.out[self.here.core, span] = line_total(line).astype(BF16)
+        ref = self.out.at[self.here.core, span]
+        for device, place, slot in self.plane(region):
+            send(ref, ref, self.ss.at[sem], self.rs.at[sem], device)
+
+    def core_back(self, region):
+        start, size, mine, landing, line, spot, axis = self.regions[region]
+        await_bytes(self.bytes_of(REGION - size), self.rs.at[8 + region])
+        ref = self.out.at[self.here.core, pl.ds(start, REGION)]
+        send(ref, ref, self.ss.at[10 + region], self.rs.at[10 + region], self.partner)
+
+    def core_done(self, region):
+        await_bytes(self.bytes_of(REGION), self.rs.at[10 + region])
 
     def bytes_of(self, count):
         return self.out.at[0, pl.ds(0, count)]
 
-    def first_back(self):
+    def small_peers(self):
         c, x, y, z = self.here.core, self.here.x, self.here.y, self.here.z
-        await_bytes(self.bytes_of((NX - 1) * YX), self.rs.at[17])
-        self.gather(self.out.at[c, rows(Y0 + y * YR, YR)], "y", 20)
-        await_bytes(self.bytes_of((NX - 1) * ZX), self.rs.at[19])
-        self.gather(self.out.at[c, rows(Z0 + z * ZR, ZR)], "z", 21)
-        await_bytes(self.bytes_of((NY - 1) * XA), self.rs.at[16])
-        await_bytes(self.bytes_of((NZ - 1) * XB), self.rs.at[18])
-        self.gather(self.out.at[c, rows(x * XR, XR)], "x", 22)
-
-    def core_back(self):
-        c = self.here.core
-        for sem, got, start, size, i in (
-            (20, (NY - 1) * YR, Y0, GROUP_Y, 25),
-            (21, (NZ - 1) * ZR, Z0, GROUP_Z, 26),
-            (22, (NX - 1) * XR, 0, GROUP_X, 24),
-        ):
-            await_bytes(self.bytes_of(got), self.rs.at[sem])
-            ref = self.out.at[c, pl.ds(start, size)]
-            send(ref, ref, self.ss.at[i], self.rs.at[i], self.partner)
-
-    def core_done(self):
-        for i, size in ((25, GROUP_Y), (26, GROUP_Z), (24, GROUP_X)):
-            await_bytes(self.bytes_of(size), self.rs.at[i])
-
-    def small_core(self):
-        send(self.small.at[1 - self.here.core], self.s_core, self.ss.at[27], self.rs.at[27], self.partner)
-
-    def small_y(self):
-        await_bytes(self.s_core, self.rs.at[27])
-        self.s_held[...] = self.small[self.here.core] + self.s_core[...]
-        self.scatter(self.s_held, 0, SR, self.s_y, "y", 7)
-
-    def small_z(self):
-        z = self.here.z
-        await_bytes(self.s_y, self.rs.at[7])
-        self.s_z[z] = total(self.s_held[rows(self.here.y * SR, SR)], self.s_y)
-        self.gather(self.s_z.at[z], "z", 11)
-
-    def small_x(self):
-        x = self.here.x
-        await_bytes(self.s_z.at[pl.ds(0, NZ - 1)], self.rs.at[11])
-        self.s_x[x] = line_total(self.s_z)
-        self.gather(self.s_x.at[x], "x", 14)
-
-    def small_back(self):
+        for dc, dy in offsets(2, NY):
+            pc, py = (c + dc) % 2, (y + dy) % NY
+            yield self.here.device(pc, x, py, z), pc, py, dc * NY + dy - 1
+
+    def small_scatter(self):
+        for device, pc, py, slot in self.small_peers():
+            send(
+                self.small.at[pc, rows(py * SR, SR)], self.s_in.at[slot], self.ss.at[12], self.rs.at[12], device
+            )
+
+    def small_plane(self):
+        c, x, y, z = self.here.core, self.here.x, self.here.y, self.here.z
+        await_bytes(self.s_in, self.rs.at[12])
+        mine = x * NZ + z
+        self.s_sum[mine] = total(self.small[c, rows(y * SR, SR)], self.s_in)
+        for device, place, slot in self.plane(1):
+            send(self.s_sum.at[mine], self.s_sum.at[mine], self.ss.at[13], self.rs.at[13], device)
+
+    def small_gather(self):
+        await_bytes(self.s_sum.at[pl.ds(0, NX * NZ - 1)], self.rs.at[13])
         place = rows(self.here.y * SR, SR)
-        await_bytes(self.s_x.at[pl.ds(0, NX - 1)], self.rs.at[14])
-        self.small_out[self.here.core, place] = line_total(self.s_x)
-        self.gather(self.small_out.at[self.here.core, place], "y", 15)
-
-    def small_core_back(self):
-        await_bytes(self.small_out.at[0, pl.ds(0, (NY - 1) * SR)], self.rs.at[15])
-        ref = self.small_out.at[self.here.core]
-        send(ref, ref, self.ss.at[23], self.rs.at[23], self.partner)
+        self.small_out[self.here.core, place] = line_total(self.s_sum)
+        ref = self.small_out.at[self.here.core, place]
+        for device, pc, py, slot in self.small_peers():
+            send(ref, ref, self.ss.at[14], self.rs.at[14], device)
 
     def small_done(self):
-        await_bytes(self.small_out.at[0], self.rs.at[23])
+        await_bytes(self.s_in, self.rs.at[14])
 
     def drain(self):
         ss = self.ss
         for k in range(4):
             await_bytes(self.core_out.at[pl.ds(0, 512)], ss.at[k])
-        for ref, i in (
-            (self.x_in, 4), (self.y_in, 5), (self.z_in, 6), (self.s_y, 7), (self.xa_in, 8), (self.xb_in, 9),
-            (self.w_in, 10), (self.s_core, 27), (self.small_out.at[0], 23),
-            (self.s_z.at[pl.ds(0, NZ - 1)], 11), (self.zz.at[pl.ds(0, NZ - 1)], 12),
-            (self.yy.at[pl.ds(0, NY - 1)], 13), (self.s_x.at[pl.ds(0, NX - 1)], 14),
-            (self.small_out.at[0, pl.ds(0, (NY - 1) * SR)], 15),
-            (self.bytes_of((NY - 1) * XA), 16), (self.bytes_of((NX - 1) * YX), 17),
-            (self.bytes_of((NZ - 1) * XB), 18), (self.bytes_of((NX - 1) * ZX), 19),
-            (self.bytes_of((NY - 1) * YR), 20), (self.bytes_of((NZ - 1) * ZR), 21),
-            (self.bytes_of((NX - 1) * XR), 22), (self.bytes_of(GROUP_X), 24), (self.bytes_of(GROUP_Y), 25),
-            (self.bytes_of(GROUP_Z), 26),
-        ):
-            await_bytes(ref, ss.at[i])
+        for region in range(2):
+            start, size, mine, landing, line, spot, axis = self.regions[region]
+            await_bytes(landing, ss.at[4 + region])
+            await_bytes(line.at[pl.ds(0, line.shape[0] - 1)], ss.at[6 + region])
+            await_bytes(self.bytes_of(REGION - size), ss.at[8 + region])
+            await_bytes(self.bytes_of(REGION), ss.at[10 + region])
+        await_bytes(self.s_in, ss.at[12])
+        await_bytes(self.s_sum.at[pl.ds(0, NX * NZ - 1)], ss.at[13])
+        await_bytes(self.s_in, ss.at[14])
 
 
 def greet(here):
     barrier = pltpu.get_barrier_semaphore()
-    mesh_id = pl.DeviceIdType.MESH
-    greeted = 0
-    for axis in ("core", "x", "y", "z"):
-        for d in steps(axis):
-            pl.semaphore_signal(barrier, inc=1, device_id=here.along(axis, d)[1], device_id_type=mesh_id)
-            greeted += 1
+    c, x, y, z = here.core, here.x, here.y, here.z
     west, east, across, across_west, across_east = halo_places(here)
-    for device in (west, east, across):
-        pl.semaphore_signal(barrier, inc=1, device_id=(device, here.lo), device_id_type=mesh_id)
-        greeted += 1
+    peers = [(device, here.lo) for device in (west, east, across)]
+    for dx, dy in offsets(NX, NY):
+        peers.append(here.device(c, (x + dx) % NX, (y + dy) % NY, z))
+    for dx, dz in offsets(NX, NZ):
+        if dz:
+            peers.append(here.device(c, (x + dx) % NX, y, (z + dz) % NZ))
+    for dy in range(NY):
+        peers.append(here.device(1 - c, x, (y + dy) % NY, z))
+    for device in peers:
+        pl.semaphore_signal(barrier, inc=1, device_id=device, device_id_type=pl.DeviceIdType.MESH)
     for device in (across_west, across_east):
 
         @pl.when(device != here.t)
         def _():
-            pl.semaphore_signal(barrier, inc=1, device_id=(device, here.lo), device_id_type=mesh_id)
-
-    return barrier, greeted, (across_west, across_east)
+            pl.semaphore_signal(
+                barrier, inc=1, device_id=(device, here.lo), device_id_type=pl.DeviceIdType.MESH
+            )
+
+    return barrier, len(peers), (across_west, across_east)
 
 
 def block_kernel(
-    owned_ref, ocean_ref, fields, grad_out, kernel, ln_gain, w_in_hbm, w_out_hbm, layer_scale,
-    state, grad_fields, wide_out, small_out,
-    band, gband, taps, conv, inverse, normed, dproj, activated, dpreact, projected, dnormed, rowsum, weight_in,
+    owned_ref, ocean_ref, fields_hbm, grad_hbm, kernel_hbm, gain_hbm, w_in_hbm, w_out_hbm, scale_hbm,
+    state_hbm, grad_fields_hbm, wide_hbm, small_hbm,
+    fields, grad_out, kernel, ln_gain, layer_scale, band, gband, taps, conv, inverse, normed, dproj, activated, dpreact, projected, dnormed, rowsum, weight_in,
     weight_out, edges, top, got, got_top, edges2, top2, got2, got_top2, small,
-    wide, core_out, core_in, held, x_in, y_in, z_in, p_out, xa_in, xb_in, r_out, r_in, zz, yy,
-    s_core, s_y, s_z, s_x, s_held, ss, rs, hs, hr, hs2, hr2, ls
+    wide, core_out, core_in, held, p_in, q_in, zz, yy, s_in, s_sum, state, grad_fields, wide_out, small_out,
+    ss, rs, hs, hr, hs2, hr2, ls, os
 ):
     here = Place()
     barrier, greeted, maybe = greet(here)
-    load_in = pltpu.make_async_copy(w_in_hbm, weight_in, ls.at[0])
-    load_out = pltpu.make_async_copy(w_out_hbm, weight_out, ls.at[1])
-    load_in.start()
-    load_out.start()
+    loads = [
+        pltpu.make_async_copy(source, target, ls.at[i])
+        for i, (source, target) in enumerate(
+            (
+                (fields_hbm, fields), (kernel_hbm, kernel), (gain_hbm, ln_gain), (scale_hbm, layer_scale),
+                (grad_hbm, grad_out), (w_in_hbm, weight_in), (w_out_hbm, weight_out),
+            )
+        )
+    ]
+    for load in loads:
+        load.start()
     reducer = Reducer(
         here,
         (
-            wide, small, wide_out, small_out, core_out, core_in, held, x_in, y_in, z_in, p_out, xa_in, xb_in,
-            r_out, r_in, zz, yy, s_core, s_y, s_z, s_x, s_held,
+            wide, small, wide_out, small_out, core_out, core_in, held, p_in, q_in, zz, yy, s_in, s_sum,
         ),
         ss,
         rs,
@@ -479,6 +447,8 @@
     lax.fori_loop(0, BAND // 64, clear, 0)
     small[...] = jnp.zeros_like(small)
     rowsum[...] = jnp.zeros_like(rowsum)
+    loads[0].wait()
+    loads[1].wait()
     for a in range(KSIZE):
         line = kernel[a].astype(F32)
         for h in range(2):
@@ -517,9 +487,11 @@
 
     lax.fori_loop(0, 2 * BLOCKS, convolve, 0)
 
+    for load in loads[2:5]:
+        load.wait()
     gain = [ln_gain[:, :128], ln_gain[:, 128:]]
     scale = [layer_scale[:, :128], layer_scale[:, 128:]]
-    STEP = 64
+    STEP = 128
 
     def norm(i, carry):
         span = rows(i * STEP, STEP)
@@ -542,8 +514,8 @@
         return carry
 
     lax.fori_loop(0, CELLS // STEP, norm, 0)
-    load_in.wait()
-    load_out.wait()
+    loads[5].wait()
+    loads[6].wait()
     across_rows = (((0,), (0,)), ((), ()))
     across_cols = (((1,), (1,)), ((), ()))
 
@@ -575,13 +547,16 @@
             wide[0, spot, :] = grad_i[:, h * 128 : (h + 1) * 128]
             wide[1, spot, :] = grad_o[:, h * 128 : (h + 1) * 128]
         reducer.core(k)
+
+        @pl.when(k == 2)
+        def _():
+            reducer.scatter(0)
+
         return carry
 
     projected[...] = jnp.zeros_like(projected)
     dnormed[...] = jnp.zeros_like(dnormed)
     lax.fori_loop(0, HID // 256, quarter, 0)
-    for region in range(3):
-        reducer.first_axis(region)
 
     def norm_back(i, carry):
         span = rows(i * STEP, STEP)
@@ -608,6 +583,7 @@
     halo_back = Halo(here, gband, edges2, top2, got2, got_top2, hs2, hr2)
     halo_back.gather_edges(owned)
     halo_back.start()
+    reducer.scatter(1)
 
     def finish_state(i, carry):
         span = rows(i * STEP, STEP)
@@ -623,7 +599,8 @@
         return carry
 
     lax.fori_loop(0, CELLS // STEP, finish_state, 0)
-    reducer.second_axis()
+    write_state = pltpu.make_async_copy(state, state_hbm, os.at[0])
+    write_state.start()
 
     def kernel_grad(i, carry):
         h, b = i // KSIZE, i % KSIZE
@@ -649,10 +626,8 @@
     for h in range(2):
         small[h, KSIZE * KSIZE : KSIZE * KSIZE + 1, :] = jnp.sum(rowsum[h], axis=0, keepdims=True)
         small[h, KSIZE * KSIZE + 1 : KSIZE * KSIZE + 2, :] = jnp.sum(rowsum[2 + h], axis=0, keepdims=True)
-    reducer.small_core()
-    reducer.third_axis()
+    reducer.small_scatter()
     halo_back.finish(owned)
-    reducer.small_y()
 
     def convolve_back(i, carry):
         h, block = i % 2, i // 2
@@ -671,20 +646,43 @@
         return carry
 
     lax.fori_loop(0, BLOCKS, convolve_back, 0)
-    reducer.second_back()
-    reducer.small_z()
+    reducer.line(0)
     lax.fori_loop(BLOCKS, 2 * BLOCKS, convolve_back, 0)
-    reducer.first_back()
-    reducer.small_x()
+    reducer.line(1)
+    reducer.small_plane()
     lax.fori_loop(0, CELLS // STEP, finish_grad, 0)
-    reducer.small_back()
-    reducer.core_back()
-    reducer.small_core_back()
-    reducer.core_done()
+    write_grad = pltpu.make_async_copy(grad_fields, grad_fields_hbm, os.at[1])
+    write_grad.start()
+    reducer.gather(0)
+    reducer.gather(1)
+    reducer.small_gather()
+    writes = [write_state, write_grad]
+    for region in range(2):
+        reducer.core_back(region)
+        span = pl.ds(region * REGION, REGION)
+        writes.append(
+            pltpu.make_async_copy(
+                wide_out.at[here.core, span], wide_hbm.at[here.core, span], os.at[2 + region]
+            )
+        )
+        writes[-1].start()
     reducer.small_done()
+    writes.append(pltpu.make_async_copy(small_out, small_hbm, os.at[4]))
+    writes[-1].start()
+    for region in range(2):
+        reducer.core_done(region)
+        span = pl.ds(region * REGION, REGION)
+        writes.append(
+            pltpu.make_async_copy(
+                wide_out.at[1 - here.core, span], wide_hbm.at[1 - here.core, span], os.at[5 + region]
+            )
+        )
+        writes[-1].start()
     reducer.drain()
     halo.drain()
     halo_back.drain()
+    for write in writes:
+        write.wait()
 
 
 def block_call(block_count, ocean, fields, grad_out, kernel, ln_gain, w_in, w_out, layer_scale):
@@ -695,6 +693,11 @@
     top = pltpu.VMEM((EDGE, SLOTS * TILE, C), BF16)
     got = pltpu.VMEM((4, EDGE, TILE, C), BF16)
     scratch = [
+        pltpu.VMEM((CELLS, C), BF16),
+        pltpu.VMEM((CELLS, C), BF16),
+        pltpu.VMEM((KSIZE, KSIZE, C), BF16),
+        pltpu.VMEM((1, C), F32),
+        pltpu.VMEM((1, C), F32),
         pltpu.VMEM((2, BAND, 128), F32),
         pltpu.VMEM((2, BAND, 128), F32),
         pltpu.VMEM((2, 56, 128), F32),
@@ -715,28 +718,24 @@
         pltpu.VMEM((HALF, 128), BF16),
         pltpu.VMEM((HALF, 128), BF16),
         pltpu.VMEM((HALF, 128), BF16),
-        pltpu.VMEM((NX - 1, XR, 128), BF16),
-        pltpu.VMEM((NY - 1, YR, 128), BF16),
-        pltpu.VMEM((NZ - 1, ZR, 128), BF16),
-        pltpu.VMEM((XR, 128), BF16),
-        pltpu.VMEM((NY - 1, XA, 128), BF16),
-        pltpu.VMEM((NZ - 1, XB, 128), BF16),
-        pltpu.VMEM((NX, YX + ZX, 128), BF16),
-        pltpu.VMEM((NX - 1, YX + ZX, 128), BF16),
-        pltpu.VMEM((NZ, XA + YX, 128), BF16),
-        pltpu.VMEM((NY, XB + ZX, 128), BF16),
-        pltpu.VMEM((SMALL, 128), F32),
-        pltpu.VMEM((NY - 1, SR, 128), F32),
-        pltpu.VMEM((NZ, SR, 128), F32),
-        pltpu.VMEM((NX, SR, 128), F32),
-        pltpu.VMEM((SMALL, 128), F32),
-        pltpu.SemaphoreType.DMA((28,)),
-        pltpu.SemaphoreType.DMA((28,)),
+        pltpu.VMEM((NX * NY - 1, PR, 128), BF16),
+        pltpu.VMEM((NX * NZ - 1, QR, 128), BF16),
+        pltpu.VMEM((NZ, PR, 128), BF16),
+        pltpu.VMEM((NY, QR, 128), BF16),
+        pltpu.VMEM((2 * NY - 1, SR, 128), F32),
+        pltpu.VMEM((NX * NZ, SR, 128), F32),
+        pltpu.VMEM((CELLS, C), BF16),
+        pltpu.VMEM((CELLS, C), BF16),
+        pltpu.VMEM((2, HALF, 128), BF16),
+        pltpu.VMEM((2, SMALL, 128), F32),
+        pltpu.SemaphoreType.DMA((15,)),
+        pltpu.SemaphoreType.DMA((15,)),
         pltpu.SemaphoreType.DMA((5,)),
         pltpu.SemaphoreType.DMA((5,)),
         pltpu.SemaphoreType.DMA((5,)),
         pltpu.SemaphoreType.DMA((5,)),
-        pltpu.SemaphoreType.DMA((2,)),
+        pltpu.SemaphoreType.DMA((7,)),
+        pltpu.SemaphoreType.DMA((7,)),
     ]
     return pl.pallas_call(
         block_kernel,
@@ -746,19 +745,108 @@
             jax.ShapeDtypeStruct((2, HALF, 128), BF16),
             jax.ShapeDtypeStruct((2, SMALL, 128), F32),
         ),
-        in_specs=[smem, smem, vmem, vmem, vmem, vmem, hbm, hbm, vmem],
-        out_specs=(vmem, vmem, vmem, vmem),
+        in_specs=[smem, smem] + [hbm] * 7,
+        out_specs=(hbm,) * 4,
         scratch_shapes=scratch,
         compiler_params=pltpu.CompilerParams(
-            collective_id=1, has_side_effects=True, vmem_limit_bytes=48 * 1024 * 1024
+            collective_id=1, has_side_effects=True, vmem_limit_bytes=56 * 1024 * 1024
         ),
     )(block_count, ocean, fields, grad_out, kernel, ln_gain, w_in, w_out, layer_scale)
+
+
+def results_kernel(
+    norm, state_hbm, fields_hbm, wide_hbm, small_hbm, state_out, fields_out, kernel_out, gain_out, in_out, out_out,
+    scale_out, state, grad_fields, wide, small, grad_in, grad_out, grad_kernel, grad_gain, grad_scale, sems, loads
+):
+    copies = [
+        pltpu.make_async_copy(state, state_out, sems.at[0]),
+        pltpu.make_async_copy(grad_fields, fields_out, sems.at[1]),
+    ]
+    through = [
+        pltpu.make_async_copy(state_hbm, state, loads.at[9]),
+        pltpu.make_async_copy(fields_hbm, grad_fields, loads.at[10]),
+    ]
+    fetches = [pltpu.make_async_copy(small_hbm, small, loads.at[8])]
+    for k in range(4):
+        for side in range(2):
+            span = pl.ds(k * 512, 512)
+            fetches.append(
+                pltpu.make_async_copy(
+                    wide_hbm.at[side, span], wide.at[side, span], loads.at[2 * k + side]
+                )
+            )
+    for copy in through + fetches:
+        copy.start()
+    for fetch, copy in zip(through, copies):
+        fetch.wait()
+        copy.start()
+    fetches[0].wait()
+    count = KSIZE * KSIZE
+    for h in range(2):
+        lanes = pl.ds(h * 128, 128)
+        for a in range(KSIZE):
+            grad_kernel[a, :, lanes] = small[h, pl.ds(a * KSIZE, KSIZE), :] * norm
+        grad_gain[:, lanes] = small[h, pl.ds(count, 1), :] * norm
+        grad_scale[:, lanes] = small[h, pl.ds(count + 1, 1), :] * norm
+    for i, (source, target) in enumerate(
+        ((grad_kernel, kernel_out), (grad_gain, gain_out), (grad_scale, scale_out))
+    ):
+        copies.append(pltpu.make_async_copy(source, target, sems.at[2 + i]))
+        copies[-1].start()
+    for k in range(4):
+        for side in range(2):
+            fetches[1 + 2 * k + side].wait()
+            for h in range(2):
+                part = wide[side, pl.ds(k * 512 + h * 256, 256), :].astype(F32) * norm
+                if side:
+                    grad_out[pl.ds(k * 256, 256), pl.ds(h * 128, 128)] = part
+                else:
+                    grad_in[:, pl.ds(k * 256 + h * 128, 128)] = part
+            if side:
+                spot = (pl.ds(k * 256, 256), slice(None))
+                source, target = grad_out, out_out
+            else:
+                spot = (slice(None), pl.ds(k * 256, 256))
+                source, target = grad_in, in_out
+            copies.append(
+                pltpu.make_async_copy(source.at[spot], target.at[spot], sems.at[5 + 2 * k + side])
+            )
+            copies[-1].start()
+    for copy in copies:
+        copy.wait()
+
+
+def results_call(norm, state, grad_fields, wide, small):
+    hbm = pl.BlockSpec(memory_space=pl.ANY)
+    sums = [((KSIZE, KSIZE, C), F32), ((1, C), F32), ((C, HID), F32), ((HID, C), F32), ((1, C), F32)]
+    return pl.pallas_call(
+        functools.partial(results_kernel, norm),
+        out_shape=tuple(
+            jax.ShapeDtypeStruct(*spec) for spec in [((CELLS, C), BF16), ((CELLS, C), BF16)] + sums
+        ),
+        in_specs=[hbm] * 4,
+        out_specs=(hbm,) * 7,
+        scratch_shapes=[
+            pltpu.VMEM((CELLS, C), BF16),
+            pltpu.VMEM((CELLS, C), BF16),
+            pltpu.VMEM((2, HALF, 128), BF16),
+            pltpu.VMEM((2, SMALL, 128), F32),
+            pltpu.VMEM((C, HID), F32),
+            pltpu.VMEM((HID, C), F32),
+            pltpu.VMEM((KSIZE, KSIZE, C), F32),
+            pltpu.VMEM((1, C), F32),
+            pltpu.VMEM((1, C), F32),
+            pltpu.SemaphoreType.DMA((13,)),
+            pltpu.SemaphoreType.DMA((11,)),
+        ],
+        compiler_params=pltpu.CompilerParams(vmem_limit_bytes=56 * 1024 * 1024),
+    )(state, grad_fields, wide, small)
 
 
 def shards(fields, grad_out, block_count, ocean, kernel, ln_gain, w_in, w_out, layer_scale):
     shape = fields.shape
     samples, slot_count, tile_rows, tile_cols, channels = shape
-    state, grad_fields, wide, small = block_call(
+    partials = block_call(
         block_count,
         ocean,
         fields.reshape(CELLS, channels),
@@ -772,18 +860,15 @@
     norm = (
         samples * lax.axis_size("dp") * slot_count * lax.axis_size("tiles") * tile_rows * tile_cols
     ) ** (-0.5)
-    taps = KSIZE * KSIZE
-    w_in_sum = jnp.transpose(wide[0].reshape(-1, channels, 128), (1, 0, 2)).reshape(channels, HID)
-    w_out_sum = jnp.transpose(wide[1].reshape(4, 2, 256, 128), (0, 2, 1, 3)).reshape(HID, channels)
-    small = jnp.concatenate([small[0], small[1]], axis=1) * norm
+    state, grad_fields, kernel_sum, gain_sum, w_in_sum, w_out_sum, scale_sum = results_call(norm, *partials)
     return (
         state.reshape(shape),
         grad_fields.reshape(shape),
-        small[:taps].reshape(KSIZE, KSIZE, channels),
-        small[taps],
-        w_in_sum.astype(F32) * norm,
-        w_out_sum.astype(F32) * norm,
-        small[taps + 1],
+        kernel_sum,
+        gain_sum.reshape(channels),
+        w_in_sum,
+        w_out_sum,
+        scale_sum.reshape(channels),
     )
 
 

time: 77.6 us -> 66 us (0.85)
  local copies, waits for them, and re-layouts: 11.1 us -> 0 us
    unnamed x19 -> x0, local copies, waits for them, and re-layouts: 8.02 us -> none
    pallas_call x0 -> x1, Pallas kernels: none -> 2.8 us  [results_call(): pl.pallas_call(functools.partial(results_kernel, norm), out_shape=tuple((...]
    pallas_call x1, Pallas kernels: 64.5 us -> 61.8 us  [block_call(): pl.pallas_call(block_kernel, out_shape=(jax.ShapeDtypeStruct((CELLS, C),...]
    mul x2 -> x0, local copies, waits for them, and re-layouts: 1.91 us -> none  [the longest x1 1.1 us: shards(): w_in_sum.astype(F32) * norm]
where the time goes in v3:
time: 66 us; the launch traced here: 65.9 us
  Pallas kernels  64.6 us (98%)
  between operations  1.29 us (2%)
    pallas_call x1, Pallas kernels, block_call(): pl.pallas_call(block_kernel, out_shape=(jax.ShapeDtypeStruct((CELLS, C),...  61.8 us
    pallas_call x1, Pallas kernels, results_call(): pl.pallas_call(functools.partial(results_kernel, norm), out_shape=tuple((...  2.8 us

profile of v3, /device:TPU:1, one launch (start us, length us, event | category | flops | bytes accessed | tf_op | source)
XLA Modules:
  0.0 65.9 jit_solution(5021448043061755697)
XLA Ops:
  1.3 61.8 %shard_map.144 = (bf16[768,256]{1,0:T(8,128)(2,1)}, bf16[768,256]{1,0:T(8,128)(2,1)}, bf16[2,2048,128]{2,1,0:T(8,128)(2,1)}, f32[2,64,128]{2,1,0:T(8,128)}) custom-call(s32[1]{0:T(128)S(6)} %copy.16.owned_ref, s32[3]{0:T(128)} %ocean_ref.1, bf16[768,256]{1,0:T(8,128)(2,1)} %bitcast.8, bf16[768,256]{1,0:T(8,128)(2,1)} %bitcast.9, ...), custom_call_target="tpu_custom_call" | custom-call | tf_op jit(solution)/shard_map/pallas_call | solution.py:740
  63.1 2.8 %shard_map.145 = (bf16[768,256]{1,0:T(8,128)(2,1)}, bf16[768,256]{1,0:T(8,128)(2,1)}, f32[7,7,256]{2,1,0:T(8,128)}, f32[1,256]{1,0:T(1,128)}, f32[256,1024]{1,0:...) custom-call(bf16[768,256]{1,0:T(8,128)(2,1)} %get-tuple-element.18.state_hbm, ...), custom_call_target="tpu_custom_call" | custom-call | tf_op jit(solution)/shard_map/pallas_call | solution.py:822

commit v4 on v3

--- a/solution.py
+++ b/solution.py
@@ -14,7 +14,8 @@
 HALF = 2048
 REGION = HALF // 2
 SMALL = 64
-PR, QR = REGION // (NX * NY), REGION // (NX * NZ)
+QUARTER = HALF // 4
+PR, QR = QUARTER // (NX * NY), QUARTER // (NX * NZ)
 SR = SMALL // NY
 F32, BF16 = jnp.float32, jnp.bfloat16
 
@@ -82,6 +83,8 @@
 
 
 def rows(start, size):
+    if isinstance(start, int):
+        return pl.ds(start, size)
     return pl.ds(pl.multiple_of(start, size), size)
 
 
@@ -221,7 +224,7 @@
     return (block // 2) * (TILE * TILE) + (block % 2) * 8
 
 
-def stencil(band, taps, h, block, backward):
+def stencil(band, taps, h, block, backward, last):
     base = LEFT - EDGE + block * 8
     total = [None] * TILE
     for b in range(KSIZE):
@@ -231,7 +234,7 @@
             turned = [
                 taps[h, pl.ds((KSIZE - 1 - a) * KSIZE + KSIZE - 1 - b, 1), :] for a in range(KSIZE)
             ]
-        for row in range(EDGE, TILE + 2 * EDGE):
+        for row in range(EDGE, last):
             window = band[h, pl.ds(row * WIDE + base + b, 8), :]
             used = straight if row >= TILE + EDGE else turned
             for a in range(KSIZE):
@@ -286,26 +289,26 @@
         self.core_out[span] = self.wide[1 - self.here.core, span].astype(BF16)
         send(self.core_out.at[span], self.core_in.at[span], self.ss.at[k], self.rs.at[k], self.partner)
 
-    def scatter(self, region):
-        start, size, mine, landing, line, spot, axis = self.regions[region]
-        sem = 4 + region
-        for k in (2 * region, 2 * region + 1):
-            await_bytes(self.core_in.at[pl.ds(0, 512)], self.rs.at[k])
-        span = pl.ds(start, REGION)
+    def scatter(self, k):
+        start, size, mine, landing, line, spot, axis = self.regions[k // 2]
+        await_bytes(self.core_in.at[pl.ds(0, QUARTER)], self.rs.at[k])
+        span = pl.ds(k * QUARTER, QUARTER)
         self.held[span] = (self.wide[self.here.core, span] + self.core_in[span].astype(F32)).astype(BF16)
-        for device, place, slot in self.plane(region):
+        for device, place, slot in self.plane(k // 2):
             send(
-                self.held.at[rows(start + place * size, size)], landing.at[slot], self.ss.at[sem], self.rs.at[sem],
-                device,
+                self.held.at[rows(k * QUARTER + place * size, size)], landing.at[k % 2, slot], self.ss.at[15 + k],
+                self.rs.at[15 + k], device,
             )
 
     def line(self, region):
         start, size, mine, landing, line, spot, axis = self.regions[region]
         sem = 6 + region
-        await_bytes(landing, self.rs.at[4 + region])
-        span = rows(start + mine * size, size)
-        own = self.wide[self.here.core, span] + self.core_in[span].astype(F32)
-        line[spot] = total(own, landing).astype(BF16)
+        for i in range(2):
+            k = 2 * region + i
+            await_bytes(landing.at[i], self.rs.at[15 + k])
+            span = rows(k * QUARTER + mine * size, size)
+            own = self.wide[self.here.core, span] + self.core_in[span].astype(F32)
+            line[spot, i * size : (i + 1) * size] = total(own, landing.at[i]).astype(BF16)
         for d in steps(axis)[::-1]:
             send(line.at[spot], line.at[spot], self.ss.at[sem], self.rs.at[sem], self.here.along(axis, d)[1])
 
@@ -313,7 +316,7 @@
         start, size, mine, landing, line, spot, axis = self.regions[region]
         sem = 8 + region
         await_bytes(line.at[pl.ds(0, line.shape[0] - 1)], self.rs.at[6 + region])
-        span = rows(start + mine * size, size)
+        span = rows(start + mine * 2 * size, 2 * size)
         self.out[self.here.core, span] = line_total(line).astype(BF16)
         ref = self.out.at[self.here.core, span]
         for device, place, slot in self.plane(region):
@@ -321,7 +324,7 @@
 
     def core_back(self, region):
         start, size, mine, landing, line, spot, axis = self.regions[region]
-        await_bytes(self.bytes_of(REGION - size), self.rs.at[8 + region])
+        await_bytes(self.bytes_of(REGION - 2 * size), self.rs.at[8 + region])
         ref = self.out.at[self.here.core, pl.ds(start, REGION)]
         send(ref, ref, self.ss.at[10 + region], self.rs.at[10 + region], self.partner)
 
@@ -368,9 +371,10 @@
             await_bytes(self.core_out.at[pl.ds(0, 512)], ss.at[k])
         for region in range(2):
             start, size, mine, landing, line, spot, axis = self.regions[region]
-            await_bytes(landing, ss.at[4 + region])
+            for i in range(2):
+                await_bytes(landing.at[i], ss.at[15 + 2 * region + i])
             await_bytes(line.at[pl.ds(0, line.shape[0] - 1)], ss.at[6 + region])
-            await_bytes(self.bytes_of(REGION - size), ss.at[8 + region])
+            await_bytes(self.bytes_of(REGION - 2 * size), ss.at[8 + region])
             await_bytes(self.bytes_of(REGION), ss.at[10 + region])
         await_bytes(self.s_in, ss.at[12])
         await_bytes(self.s_sum.at[pl.ds(0, NX * NZ - 1)], ss.at[13])
@@ -462,7 +466,7 @@
         band[1, place, :] = line[:, 128:]
         return carry
 
-    lax.fori_loop(0, SLOTS * TILE, fill, 0)
+    lax.fori_loop(0, SLOTS * TILE, fill, 0, unroll=4)
     halo = Halo(here, band, edges, top, got, got_top, hs, hr)
     halo.gather_edges(owned)
     at_seam = jnp.logical_or(maybe[0] == here.t, maybe[1] == here.t)
@@ -476,16 +480,65 @@
         pl.semaphore_wait(barrier, greeted + 2)
 
     halo.start()
-    halo.finish(owned)
 
     def convolve(i, carry):
         h, block = i // BLOCKS, i % BLOCKS
-        result = stencil(band, taps, h, block, False)
+        result = stencil(band, taps, h, block, False, TILE + EDGE)
         for r in range(TILE):
             conv[h, pl.ds(pl.multiple_of(block_start(block) + r * TILE, 8), 8), :] = result[r]
         return carry
 
     lax.fori_loop(0, 2 * BLOCKS, convolve, 0)
+
+    halo.finish(owned)
+
+    def add_fold(i, carry):
+        h, block = i // BLOCKS, i % BLOCKS
+        base = LEFT - EDGE + block * 8
+        sums = [None] * EDGE
+        for b in range(KSIZE):
+            for row in range(TILE + EDGE, TILE + 2 * EDGE):
+                window = band[h, pl.ds(row * WIDE + base + b, 8), :]
+                for a in range(row - TILE + 1, KSIZE):
+                    term = taps[h, pl.ds(a * KSIZE + b, 1), :] * window
+                    r = row - a - TILE + EDGE
+                    sums[r] = term if sums[r] is None else sums[r] + term
+        for r in range(EDGE):
+            place = pl.ds(pl.multiple_of(block_start(block) + (TILE - EDGE + r) * TILE, 8), 8)
+            conv[h, place, :] = conv[h, place, :] + sums[r]
+        return carry
+
+    lax.fori_loop(0, 2 * BLOCKS, add_fold, 0, unroll=3)
+    sub = lax.broadcasted_iota(jnp.int32, (8, 128), 0)
+
+    def edge_sums(h, base, shifts, held):
+        sums = [None] * TILE
+        for b in shifts:
+            weights = [taps[h, pl.ds(a * KSIZE + b, 1), :] for a in range(KSIZE)]
+            for row in range(EDGE, TILE + EDGE):
+                window = jnp.where(held(b), band[h, pl.ds(row * WIDE + base + b, 8), :], 0.0)
+                for a in range(KSIZE):
+                    r = row - a
+                    if 0 <= r < TILE:
+                        term = weights[a] * window
+                        sums[r] = term if sums[r] is None else sums[r] + term
+        return sums
+
+    def add_edges(h, carry):
+        west = edge_sums(h, LEFT - EDGE, range(EDGE), lambda b: sub < EDGE - b)
+        for r in range(TILE):
+            place = pl.ds(r * TILE, 8)
+            conv[h, place, :] = conv[h, place, :] + west[r]
+        east = edge_sums(
+            h, LEFT - EDGE + owned * TILE - 8, range(EDGE + 1, KSIZE), lambda b: sub >= 8 + EDGE - b
+        )
+        for n in range(1, SLOTS + 1):
+            for r in range(TILE):
+                place = pl.ds((n - 1) * TILE * TILE + r * TILE + 8, 8)
+                conv[h, place, :] = conv[h, place, :] + jnp.where(owned == n, east[r], 0.0)
+        return carry
+
+    lax.fori_loop(0, 2, add_edges, 0, unroll=2)
 
     for load in loads[2:5]:
         load.wait()
@@ -513,14 +566,15 @@
             dproj[span, lanes] = (mask * scale[h] * cotangent).astype(BF16)
         return carry
 
-    lax.fori_loop(0, CELLS // STEP, norm, 0)
+    lax.fori_loop(0, CELLS // STEP, norm, 0, unroll=2)
     loads[5].wait()
     loads[6].wait()
     across_rows = (((0,), (0,)), ((), ()))
     across_cols = (((1,), (1,)), ((), ()))
 
     def quarter(k, carry):
-        part_in = weight_in[:, rows(k * 256, 256)]
+        hidden = rows(k * 256, 256)
+        part_in = weight_in[:, hidden]
         part_out = weight_out[rows(k * 256, 256), :]
         for m in range(SLOTS):
             span = pl.ds(m * 256, 256)
@@ -533,15 +587,14 @@
             act = (v * half).astype(BF16)
             slope = half + (v * half) * (1.0 - t) * (GELU_A + (3.0 * GELU_A * GELU_B) * square)
             dpre = (dact * slope).astype(BF16)
-            activated[span, :] = act
-            dpreact[span, :] = dpre
-            forward = jnp.dot(act, part_out, preferred_element_type=F32)
-            back = lax.dot_general(dpre, part_in, across_cols, preferred_element_type=F32)
-            first = k == 0
-            projected[span, :] = jnp.where(first, forward, projected[span, :] + forward)
-            dnormed[span, :] = jnp.where(first, back, dnormed[span, :] + back)
-        grad_o = lax.dot_general(activated[...], dproj[...], across_rows, preferred_element_type=F32)
-        grad_i = lax.dot_general(normed[...], dpreact[...], across_rows, preferred_element_type=F32)
+            activated[span, hidden] = act
+            dpreact[span, hidden] = dpre
+        grad_o = lax.dot_general(
+            activated[:, hidden], dproj[...], across_rows, preferred_element_type=F32
+        )
+        grad_i = lax.dot_general(
+            normed[...], dpreact[:, hidden], across_rows, preferred_element_type=F32
+        )
         for h in range(2):
             spot = rows(k * 512 + h * 256, 256)
             wide[0, spot, :] = grad_i[:, h * 128 : (h + 1) * 128]
@@ -551,12 +604,21 @@
         @pl.when(k == 2)
         def _():
             reducer.scatter(0)
-
-        return carry
-
-    projected[...] = jnp.zeros_like(projected)
-    dnormed[...] = jnp.zeros_like(dnormed)
-    lax.fori_loop(0, HID // 256, quarter, 0)
+            reducer.scatter(1)
+
+        @pl.when(k == 3)
+        def _():
+            reducer.scatter(2)
+
+        return carry
+
+    for k in range(HID // 256):
+        quarter(k, 0)
+    for m in range(SLOTS):
+        span = pl.ds(m * 256, 256)
+        dnormed[span, :] = lax.dot_general(
+            dpreact[span, :], weight_in[...], across_cols, preferred_element_type=F32
+        )
 
     def norm_back(i, carry):
         span = rows(i * STEP, STEP)
@@ -579,11 +641,15 @@
                 gband[h, place, :] = grad[q * TILE : (q + 1) * TILE]
         return carry
 
-    lax.fori_loop(0, CELLS // STEP, norm_back, 0)
+    lax.fori_loop(0, CELLS // STEP, norm_back, 0, unroll=2)
     halo_back = Halo(here, gband, edges2, top2, got2, got_top2, hs2, hr2)
     halo_back.gather_edges(owned)
     halo_back.start()
-    reducer.scatter(1)
+    reducer.scatter(3)
+
+    for m in range(SLOTS):
+        span = pl.ds(m * 256, 256)
+        projected[span, :] = jnp.dot(activated[span, :], weight_out[...], preferred_element_type=F32)
 
     def finish_state(i, carry):
         span = rows(i * STEP, STEP)
@@ -598,7 +664,7 @@
             state[span, lanes] = (mask * (kept + scale[h] * out)).astype(BF16)
         return carry
 
-    lax.fori_loop(0, CELLS // STEP, finish_state, 0)
+    lax.fori_loop(0, CELLS // STEP, finish_state, 0, unroll=2)
     write_state = pltpu.make_async_copy(state, state_hbm, os.at[0])
     write_state.start()
 
@@ -631,7 +697,7 @@
 
     def convolve_back(i, carry):
         h, block = i % 2, i // 2
-        result = stencil(gband, taps, h, block, True)
+        result = stencil(gband, taps, h, block, True, TILE + 2 * EDGE)
         for r in range(TILE):
             conv[h, pl.ds(pl.multiple_of(block_start(block) + r * TILE, 8), 8), :] = result[r]
         return carry
@@ -645,10 +711,11 @@
             grad_fields[span, lanes] = grad.astype(BF16)
         return carry
 
-    lax.fori_loop(0, BLOCKS, convolve_back, 0)
+    lax.fori_loop(0, 6, convolve_back, 0)
     reducer.line(0)
-    lax.fori_loop(BLOCKS, 2 * BLOCKS, convolve_back, 0)
+    lax.fori_loop(6, 8, convolve_back, 0)
     reducer.line(1)
+    lax.fori_loop(8, 2 * BLOCKS, convolve_back, 0)
     reducer.small_plane()
     lax.fori_loop(0, CELLS // STEP, finish_grad, 0)
     write_grad = pltpu.make_async_copy(grad_fields, grad_fields_hbm, os.at[1])
@@ -705,8 +772,8 @@
         pltpu.VMEM((CELLS, 128), F32),
         pltpu.VMEM((CELLS, C), BF16),
         pltpu.VMEM((CELLS, C), BF16),
-        pltpu.VMEM((CELLS, 256), BF16),
-        pltpu.VMEM((CELLS, 256), BF16),
+        pltpu.VMEM((CELLS, HID), BF16),
+        pltpu.VMEM((CELLS, HID), BF16),
         pltpu.VMEM((CELLS, C), F32),
         pltpu.VMEM((CELLS, C), F32),
         pltpu.VMEM((4, 8, 128), F32),
@@ -718,18 +785,18 @@
         pltpu.VMEM((HALF, 128), BF16),
         pltpu.VMEM((HALF, 128), BF16),
         pltpu.VMEM((HALF, 128), BF16),
-        pltpu.VMEM((NX * NY - 1, PR, 128), BF16),
-        pltpu.VMEM((NX * NZ - 1, QR, 128), BF16),
-        pltpu.VMEM((NZ, PR, 128), BF16),
-        pltpu.VMEM((NY, QR, 128), BF16),
+        pltpu.VMEM((2, NX * NY - 1, PR, 128), BF16),
+        pltpu.VMEM((2, NX * NZ - 1, QR, 128), BF16),
+        pltpu.VMEM((NZ, 2 * PR, 128), BF16),
+        pltpu.VMEM((NY, 2 * QR, 128), BF16),
         pltpu.VMEM((2 * NY - 1, SR, 128), F32),
         pltpu.VMEM((NX * NZ, SR, 128), F32),
         pltpu.VMEM((CELLS, C), BF16),
         pltpu.VMEM((CELLS, C), BF16),
         pltpu.VMEM((2, HALF, 128), BF16),
         pltpu.VMEM((2, SMALL, 128), F32),
-        pltpu.SemaphoreType.DMA((15,)),
-        pltpu.SemaphoreType.DMA((15,)),
+        pltpu.SemaphoreType.DMA((19,)),
+        pltpu.SemaphoreType.DMA((19,)),
         pltpu.SemaphoreType.DMA((5,)),
         pltpu.SemaphoreType.DMA((5,)),
         pltpu.SemaphoreType.DMA((5,)),
@@ -754,6 +821,14 @@
     )(block_count, ocean, fields, grad_out, kernel, ln_gain, w_in, w_out, layer_scale)
 
 
+def quarter_rows(wide, side, k):
+    size = QR if k // 2 else PR
+    start = (k // 2) * REGION + (k % 2) * size
+    return jnp.concatenate(
+        [wide[side, pl.ds(start + i * 2 * size, size), :] for i in range(QUARTER // size)], axis=0
+    )
+
+
 def results_kernel(
     norm, state_hbm, fields_hbm, wide_hbm, small_hbm, state_out, fields_out, kernel_out, gain_out, in_out, out_out,
     scale_out, state, grad_fields, wide, small, grad_in, grad_out, grad_kernel, grad_gain, grad_scale, sems, loads
@@ -769,12 +844,13 @@
     fetches = [pltpu.make_async_copy(small_hbm, small, loads.at[8])]
     for k in range(4):
         for side in range(2):
-            span = pl.ds(k * 512, 512)
-            fetches.append(
-                pltpu.make_async_copy(
-                    wide_hbm.at[side, span], wide.at[side, span], loads.at[2 * k + side]
+            if k % 2 == 0:
+                span = pl.ds(k * QUARTER, REGION)
+                fetches.append(
+                    pltpu.make_async_copy(
+                        wide_hbm.at[side, span], wide.at[side, span], loads.at[k + side]
+                    )
                 )
-            )
     for copy in through + fetches:
         copy.start()
     for fetch, copy in zip(through, copies):
@@ -795,9 +871,10 @@
         copies[-1].start()
     for k in range(4):
         for side in range(2):
-            fetches[1 + 2 * k + side].wait()
+            if k % 2 == 0:
+                fetches[1 + k + side].wait()
             for h in range(2):
-                part = wide[side, pl.ds(k * 512 + h * 256, 256), :].astype(F32) * norm
+                part = quarter_rows(wide, side, k)[h * 256 : (h + 1) * 256].astype(F32) * norm
                 if side:
                     grad_out[pl.ds(k * 256, 256), pl.ds(h * 128, 128)] = part
                 else:

time: 66 us -> 61.6 us (0.933)
  Pallas kernels: 64.6 us -> 60.1 us
    pallas_call x1, Pallas kernels: 61.8 us -> 57.3 us  [block_call(): pl.pallas_call(block_kernel, out_shape=(jax.ShapeDtypeStruct((CELLS, C),...]
where the time goes in v4:
time: 61.6 us; the launch traced here: 61.4 us
  Pallas kernels  60.1 us (98%)
  between operations  1.29 us (2%)
    pallas_call x1, Pallas kernels, block_call(): pl.pallas_call(block_kernel, out_shape=(jax.ShapeDtypeStruct((CELLS, C),...  57.3 us
    pallas_call x1, Pallas kernels, results_call(): pl.pallas_call(functools.partial(results_kernel, norm), out_shape=tuple((...  2.8 us

profile of v4, /device:TPU:1, one launch (start us, length us, event | category | flops | bytes accessed | tf_op | source)
XLA Modules:
  0.0 61.4 jit_solution(11821647694793866993)
XLA Ops:
  1.3 57.3 %shard_map.144 = (bf16[768,256]{1,0:T(8,128)(2,1)}, bf16[768,256]{1,0:T(8,128)(2,1)}, bf16[2,2048,128]{2,1,0:T(8,128)(2,1)}, f32[2,64,128]{2,1,0:T(8,128)}) custom-call(s32[1]{0:T(128)S(6)} %copy.16.owned_ref, s32[3]{0:T(128)} %ocean_ref.1, bf16[768,256]{1,0:T(8,128)(2,1)} %bitcast.8, bf16[768,256]{1,0:T(8,128)(2,1)} %bitcast.9, ...), custom_call_target="tpu_custom_call" | custom-call | tf_op jit(solution)/shard_map/pallas_call | solution.py:807
  58.6 2.8 %shard_map.145 = (bf16[768,256]{1,0:T(8,128)(2,1)}, bf16[768,256]{1,0:T(8,128)(2,1)}, f32[7,7,256]{2,1,0:T(8,128)}, f32[1,256]{1,0:T(1,128)}, f32[256,1024]{1,0:...) custom-call(bf16[768,256]{1,0:T(8,128)(2,1)} %get-tuple-element.18.state_hbm, ...), custom_call_target="tpu_custom_call" | custom-call | tf_op jit(solution)/shard_map/pallas_call | solution.py:899

commit v5 on v4

--- a/solution.py
+++ b/solution.py
@@ -12,7 +12,6 @@
 NX, NZ, NYH = 4, 8, 4
 NY = 2 * NYH
 HALF = 2048
-REGION = HALF // 2
 SMALL = 64
 QUARTER = HALF // 4
 PR, QR = QUARTER // (NX * NY), QUARTER // (NX * NZ)
@@ -267,17 +266,17 @@
         ) = refs
         c, x, y, z = here.core, here.x, here.y, here.z
         self.partner = here.device(1 - c, x, y, z)
-        self.regions = (
-            (0, PR, x * NY + y, self.p_in, self.zz, z, "z"),
-            (REGION, QR, x * NZ + z, self.q_in, self.yy, y, "y"),
+        self.quarters = tuple(
+            (PR, x * NY + y, self.p_in, self.zz, z, "z") if k % 2 == 0 else (QR, x * NZ + z, self.q_in, self.yy, y, "y")
+            for k in range(4)
         )
 
-    def plane(self, region):
+    def plane(self, side):
         c, x, y, z = self.here.core, self.here.x, self.here.y, self.here.z
-        n = NZ if region else NY
+        n = NZ if side else NY
         for dx, d in offsets(NX, n):
             px = (x + dx) % NX
-            if region:
+            if side:
                 pz = (z + d) % NZ
                 yield self.here.device(c, px, y, pz), px * NZ + pz, dx * n + d - 1
             else:
@@ -285,51 +284,48 @@
                 yield self.here.device(c, px, py, z), px * NY + py, dx * n + d - 1
 
     def core(self, k):
-        span = rows(k * 512, 512)
+        span = rows(k * QUARTER, QUARTER)
         self.core_out[span] = self.wide[1 - self.here.core, span].astype(BF16)
         send(self.core_out.at[span], self.core_in.at[span], self.ss.at[k], self.rs.at[k], self.partner)
 
     def scatter(self, k):
-        start, size, mine, landing, line, spot, axis = self.regions[k // 2]
+        size, mine, landing, line, spot, axis = self.quarters[k]
         await_bytes(self.core_in.at[pl.ds(0, QUARTER)], self.rs.at[k])
         span = pl.ds(k * QUARTER, QUARTER)
         self.held[span] = (self.wide[self.here.core, span] + self.core_in[span].astype(F32)).astype(BF16)
-        for device, place, slot in self.plane(k // 2):
+        for device, place, slot in self.plane(k % 2):
             send(
-                self.held.at[rows(k * QUARTER + place * size, size)], landing.at[k % 2, slot], self.ss.at[15 + k],
-                self.rs.at[15 + k], device,
+                self.held.at[rows(k * QUARTER + place * size, size)], landing.at[k // 2, slot], self.ss.at[4 + k],
+                self.rs.at[4 + k], device,
             )
 
-    def line(self, region):
-        start, size, mine, landing, line, spot, axis = self.regions[region]
-        sem = 6 + region
-        for i in range(2):
-            k = 2 * region + i
-            await_bytes(landing.at[i], self.rs.at[15 + k])
-            span = rows(k * QUARTER + mine * size, size)
-            own = self.wide[self.here.core, span] + self.core_in[span].astype(F32)
-            line[spot, i * size : (i + 1) * size] = total(own, landing.at[i]).astype(BF16)
+    def line(self, k):
+        size, mine, landing, line, spot, axis = self.quarters[k]
+        await_bytes(landing.at[k // 2], self.rs.at[4 + k])
+        span = rows(k * QUARTER + mine * size, size)
+        own = self.wide[self.here.core, span] + self.core_in[span].astype(F32)
+        line[k // 2, spot] = total(own, landing.at[k // 2]).astype(BF16)
+        ref = line.at[k // 2, spot]
         for d in steps(axis)[::-1]:
-            send(line.at[spot], line.at[spot], self.ss.at[sem], self.rs.at[sem], self.here.along(axis, d)[1])
-
-    def gather(self, region):
-        start, size, mine, landing, line, spot, axis = self.regions[region]
-        sem = 8 + region
-        await_bytes(line.at[pl.ds(0, line.shape[0] - 1)], self.rs.at[6 + region])
-        span = rows(start + mine * 2 * size, 2 * size)
-        self.out[self.here.core, span] = line_total(line).astype(BF16)
+            send(ref, ref, self.ss.at[8 + k], self.rs.at[8 + k], self.here.along(axis, d)[1])
+
+    def gather(self, k):
+        size, mine, landing, line, spot, axis = self.quarters[k]
+        await_bytes(line.at[0, pl.ds(0, line.shape[1] - 1)], self.rs.at[8 + k])
+        span = rows(k * QUARTER + mine * size, size)
+        self.out[self.here.core, span] = line_total(line.at[k // 2]).astype(BF16)
         ref = self.out.at[self.here.core, span]
-        for device, place, slot in self.plane(region):
-            send(ref, ref, self.ss.at[sem], self.rs.at[sem], device)
-
-    def core_back(self, region):
-        start, size, mine, landing, line, spot, axis = self.regions[region]
-        await_bytes(self.bytes_of(REGION - 2 * size), self.rs.at[8 + region])
-        ref = self.out.at[self.here.core, pl.ds(start, REGION)]
-        send(ref, ref, self.ss.at[10 + region], self.rs.at[10 + region], self.partner)
-
-    def core_done(self, region):
-        await_bytes(self.bytes_of(REGION), self.rs.at[10 + region])
+        for device, place, slot in self.plane(k % 2):
+            send(ref, ref, self.ss.at[12 + k], self.rs.at[12 + k], device)
+
+    def core_back(self, k):
+        size = self.quarters[k][0]
+        await_bytes(self.bytes_of(QUARTER - size), self.rs.at[12 + k])
+        ref = self.out.at[self.here.core, pl.ds(k * QUARTER, QUARTER)]
+        send(ref, ref, self.ss.at[16 + k], self.rs.at[16 + k], self.partner)
+
+    def core_done(self, k):
+        await_bytes(self.bytes_of(QUARTER), self.rs.at[16 + k])
 
     def bytes_of(self, count):
         return self.out.at[0, pl.ds(0, count)]
@@ -343,42 +339,40 @@
     def small_scatter(self):
         for device, pc, py, slot in self.small_peers():
             send(
-                self.small.at[pc, rows(py * SR, SR)], self.s_in.at[slot], self.ss.at[12], self.rs.at[12], device
+                self.small.at[pc, rows(py * SR, SR)], self.s_in.at[slot], self.ss.at[20], self.rs.at[20], device
             )
 
     def small_plane(self):
         c, x, y, z = self.here.core, self.here.x, self.here.y, self.here.z
-        await_bytes(self.s_in, self.rs.at[12])
+        await_bytes(self.s_in, self.rs.at[20])
         mine = x * NZ + z
         self.s_sum[mine] = total(self.small[c, rows(y * SR, SR)], self.s_in)
         for device, place, slot in self.plane(1):
-            send(self.s_sum.at[mine], self.s_sum.at[mine], self.ss.at[13], self.rs.at[13], device)
+            send(self.s_sum.at[mine], self.s_sum.at[mine], self.ss.at[21], self.rs.at[21], device)
 
     def small_gather(self):
-        await_bytes(self.s_sum.at[pl.ds(0, NX * NZ - 1)], self.rs.at[13])
+        await_bytes(self.s_sum.at[pl.ds(0, NX * NZ - 1)], self.rs.at[21])
         place = rows(self.here.y * SR, SR)
         self.small_out[self.here.core, place] = line_total(self.s_sum)
         ref = self.small_out.at[self.here.core, place]
         for device, pc, py, slot in self.small_peers():
-            send(ref, ref, self.ss.at[14], self.rs.at[14], device)
+            send(ref, ref, self.ss.at[22], self.rs.at[22], device)
 
     def small_done(self):
-        await_bytes(self.s_in, self.rs.at[14])
+        await_bytes(self.s_in, self.rs.at[22])
 
     def drain(self):
         ss = self.ss
         for k in range(4):
-            await_bytes(self.core_out.at[pl.ds(0, 512)], ss.at[k])
-        for region in range(2):
-            start, size, mine, landing, line, spot, axis = self.regions[region]
-            for i in range(2):
-                await_bytes(landing.at[i], ss.at[15 + 2 * region + i])
-            await_bytes(line.at[pl.ds(0, line.shape[0] - 1)], ss.at[6 + region])
-            await_bytes(self.bytes_of(REGION - 2 * size), ss.at[8 + region])
-            await_bytes(self.bytes_of(REGION), ss.at[10 + region])
-        await_bytes(self.s_in, ss.at[12])
-        await_bytes(self.s_sum.at[pl.ds(0, NX * NZ - 1)], ss.at[13])
-        await_bytes(self.s_in, ss.at[14])
+            size, mine, landing, line, spot, axis = self.quarters[k]
+            await_bytes(self.core_out.at[pl.ds(0, QUARTER)], ss.at[k])
+            await_bytes(landing.at[k // 2], ss.at[4 + k])
+            await_bytes(line.at[0, pl.ds(0, line.shape[1] - 1)], ss.at[8 + k])
+            await_bytes(self.bytes_of(QUARTER - size), ss.at[12 + k])
+            await_bytes(self.bytes_of(QUARTER), ss.at[16 + k])
+        await_bytes(self.s_in, ss.at[20])
+        await_bytes(self.s_sum.at[pl.ds(0, NX * NZ - 1)], ss.at[21])
+        await_bytes(self.s_in, ss.at[22])
 
 
 def greet(here):
@@ -601,14 +595,8 @@
             wide[1, spot, :] = grad_o[:, h * 128 : (h + 1) * 128]
         reducer.core(k)
 
-        @pl.when(k == 2)
-        def _():
-            reducer.scatter(0)
-            reducer.scatter(1)
-
-        @pl.when(k == 3)
-        def _():
-            reducer.scatter(2)
+        if k >= 2:
+            reducer.scatter(k - 2)
 
         return carry
 
@@ -619,6 +607,8 @@
         dnormed[span, :] = lax.dot_general(
             dpreact[span, :], weight_in[...], across_cols, preferred_element_type=F32
         )
+
+    reducer.scatter(2)
 
     def norm_back(i, carry):
         span = rows(i * STEP, STEP)
@@ -643,9 +633,9 @@
 
     lax.fori_loop(0, CELLS // STEP, norm_back, 0, unroll=2)
     halo_back = Halo(here, gband, edges2, top2, got2, got_top2, hs2, hr2)
+    reducer.scatter(3)
     halo_back.gather_edges(owned)
     halo_back.start()
-    reducer.scatter(3)
 
     for m in range(SLOTS):
         span = pl.ds(m * 256, 256)
@@ -683,7 +673,7 @@
             return tuple(sums)
 
         zero = tuple(jnp.zeros((8, 128), F32) for a in range(KSIZE))
-        sums = lax.fori_loop(0, BLOCKS, one_block, zero)
+        sums = lax.fori_loop(0, BLOCKS, one_block, zero, unroll=3)
         for a in range(KSIZE):
             small[h, pl.ds(a * KSIZE + b, 1), :] = jnp.sum(sums[a], axis=0, keepdims=True)
         return carry
@@ -693,6 +683,8 @@
         small[h, KSIZE * KSIZE : KSIZE * KSIZE + 1, :] = jnp.sum(rowsum[h], axis=0, keepdims=True)
         small[h, KSIZE * KSIZE + 1 : KSIZE * KSIZE + 2, :] = jnp.sum(rowsum[2 + h], axis=0, keepdims=True)
     reducer.small_scatter()
+    for k in range(3):
+        reducer.line(k)
     halo_back.finish(owned)
 
     def convolve_back(i, carry):
@@ -711,40 +703,36 @@
             grad_fields[span, lanes] = grad.astype(BF16)
         return carry
 
-    lax.fori_loop(0, 6, convolve_back, 0)
-    reducer.line(0)
-    lax.fori_loop(6, 8, convolve_back, 0)
-    reducer.line(1)
-    lax.fori_loop(8, 2 * BLOCKS, convolve_back, 0)
+    lax.fori_loop(0, 2, convolve_back, 0)
+    reducer.line(3)
+    lax.fori_loop(2, 2 * BLOCKS, convolve_back, 0)
     reducer.small_plane()
+    for k in range(4):
+        reducer.gather(k)
     lax.fori_loop(0, CELLS // STEP, finish_grad, 0)
     write_grad = pltpu.make_async_copy(grad_fields, grad_fields_hbm, os.at[1])
     write_grad.start()
-    reducer.gather(0)
-    reducer.gather(1)
     reducer.small_gather()
     writes = [write_state, write_grad]
-    for region in range(2):
-        reducer.core_back(region)
-        span = pl.ds(region * REGION, REGION)
+    for k in range(4):
+        reducer.core_back(k)
+        span = pl.ds(k * QUARTER, QUARTER)
+        writes.append(
+            pltpu.make_async_copy(wide_out.at[here.core, span], wide_hbm.at[here.core, span], os.at[2 + k])
+        )
+        writes[-1].start()
+    for k in range(4):
+        reducer.core_done(k)
+        span = pl.ds(k * QUARTER, QUARTER)
         writes.append(
             pltpu.make_async_copy(
-                wide_out.at[here.core, span], wide_hbm.at[here.core, span], os.at[2 + region]
+                wide_out.at[1 - here.core, span], wide_hbm.at[1 - here.core, span], os.at[7 + k]
             )
         )
         writes[-1].start()
     reducer.small_done()
-    writes.append(pltpu.make_async_copy(small_out, small_hbm, os.at[4]))
+    writes.append(pltpu.make_async_copy(small_out, small_hbm, os.at[6]))
     writes[-1].start()
-    for region in range(2):
-        reducer.core_done(region)
-        span = pl.ds(region * REGION, REGION)
-        writes.append(
-            pltpu.make_async_copy(
-                wide_out.at[1 - here.core, span], wide_hbm.at[1 - here.core, span], os.at[5 + region]
-            )
-        )
-        writes[-1].start()
     reducer.drain()
     halo.drain()
     halo_back.drain()
@@ -787,22 +775,22 @@
         pltpu.VMEM((HALF, 128), BF16),
         pltpu.VMEM((2, NX * NY - 1, PR, 128), BF16),
         pltpu.VMEM((2, NX * NZ - 1, QR, 128), BF16),
-        pltpu.VMEM((NZ, 2 * PR, 128), BF16),
-        pltpu.VMEM((NY, 2 * QR, 128), BF16),
+        pltpu.VMEM((2, NZ, PR, 128), BF16),
+        pltpu.VMEM((2, NY, QR, 128), BF16),
         pltpu.VMEM((2 * NY - 1, SR, 128), F32),
         pltpu.VMEM((NX * NZ, SR, 128), F32),
         pltpu.VMEM((CELLS, C), BF16),
         pltpu.VMEM((CELLS, C), BF16),
         pltpu.VMEM((2, HALF, 128), BF16),
         pltpu.VMEM((2, SMALL, 128), F32),
-        pltpu.SemaphoreType.DMA((19,)),
-        pltpu.SemaphoreType.DMA((19,)),
+        pltpu.SemaphoreType.DMA((23,)),
+        pltpu.SemaphoreType.DMA((23,)),
         pltpu.SemaphoreType.DMA((5,)),
         pltpu.SemaphoreType.DMA((5,)),
         pltpu.SemaphoreType.DMA((5,)),
         pltpu.SemaphoreType.DMA((5,)),
         pltpu.SemaphoreType.DMA((7,)),
-        pltpu.SemaphoreType.DMA((7,)),
+        pltpu.SemaphoreType.DMA((11,)),
     ]
     return pl.pallas_call(
         block_kernel,
@@ -821,14 +809,6 @@
     )(block_count, ocean, fields, grad_out, kernel, ln_gain, w_in, w_out, layer_scale)
 
 
-def quarter_rows(wide, side, k):
-    size = QR if k // 2 else PR
-    start = (k // 2) * REGION + (k % 2) * size
-    return jnp.concatenate(
-        [wide[side, pl.ds(start + i * 2 * size, size), :] for i in range(QUARTER // size)], axis=0
-    )
-
-
 def results_kernel(
     norm, state_hbm, fields_hbm, wide_hbm, small_hbm, state_out, fields_out, kernel_out, gain_out, in_out, out_out,
     scale_out, state, grad_fields, wide, small, grad_in, grad_out, grad_kernel, grad_gain, grad_scale, sems, loads
@@ -844,13 +824,12 @@
     fetches = [pltpu.make_async_copy(small_hbm, small, loads.at[8])]
     for k in range(4):
         for side in range(2):
-            if k % 2 == 0:
-                span = pl.ds(k * QUARTER, REGION)
-                fetches.append(
-                    pltpu.make_async_copy(
-                        wide_hbm.at[side, span], wide.at[side, span], loads.at[k + side]
-                    )
+            span = pl.ds(k * QUARTER, QUARTER)
+            fetches.append(
+                pltpu.make_async_copy(
+                    wide_hbm.at[side, span], wide.at[side, span], loads.at[2 * k + side]
                 )
+            )
     for copy in through + fetches:
         copy.start()
     for fetch, copy in zip(through, copies):
@@ -871,10 +850,9 @@
         copies[-1].start()
     for k in range(4):
         for side in range(2):
-            if k % 2 == 0:
-                fetches[1 + k + side].wait()
+            fetches[1 + 2 * k + side].wait()
             for h in range(2):
-                part = quarter_rows(wide, side, k)[h * 256 : (h + 1) * 256].astype(F32) * norm
+                part = wide[side, pl.ds(k * 512 + h * 256, 256), :].astype(F32) * norm
                 if side:
                     grad_out[pl.ds(k * 256, 256), pl.ds(h * 128, 128)] = part
                 else:

time: 61.6 us -> 61.3 us (level)
  no operation moved by 1% of the time
where the time goes in v5:
time: 61.3 us; the launch traced here: 61.1 us
  Pallas kernels  59.8 us (98%)
  between operations  1.29 us (2%)
    pallas_call x1, Pallas kernels, block_call(): pl.pallas_call(block_kernel, out_shape=(jax.ShapeDtypeStruct((CELLS, C),...  57 us
    pallas_call x1, Pallas kernels, results_call(): pl.pallas_call(functools.partial(results_kernel, norm), out_shape=tuple((...  2.8 us

profile of v5, /device:TPU:1, one launch (start us, length us, event | category | flops | bytes accessed | tf_op | source)
XLA Modules:
  0.0 61.1 jit_solution(16729844939146349774)
XLA Ops:
  1.3 57.0 %shard_map.144 = (bf16[768,256]{1,0:T(8,128)(2,1)}, bf16[768,256]{1,0:T(8,128)(2,1)}, bf16[2,2048,128]{2,1,0:T(8,128)(2,1)}, f32[2,64,128]{2,1,0:T(8,128)}) custom-call(s32[1]{0:T(128)S(6)} %copy.16.owned_ref, s32[3]{0:T(128)} %ocean_ref.1, bf16[768,256]{1,0:T(8,128)(2,1)} %bitcast.8, bf16[768,256]{1,0:T(8,128)(2,1)} %bitcast.9, ...), custom_call_target="tpu_custom_call" | custom-call | tf_op jit(solution)/shard_map/pallas_call | solution.py:795
  58.3 2.8 %shard_map.145 = (bf16[768,256]{1,0:T(8,128)(2,1)}, bf16[768,256]{1,0:T(8,128)(2,1)}, f32[7,7,256]{2,1,0:T(8,128)}, f32[1,256]{1,0:T(1,128)}, f32[256,1024]{1,0:...) custom-call(bf16[768,256]{1,0:T(8,128)(2,1)} %get-tuple-element.18.state_hbm, ...), custom_call_target="tpu_custom_call" | custom-call | tf_op jit(solution)/shard_map/pallas_call | solution.py:877

commit v6 on v5

--- a/solution.py
+++ b/solution.py
@@ -602,13 +602,14 @@
 
     for k in range(HID // 256):
         quarter(k, 0)
+    reducer.scatter(2)
     for m in range(SLOTS):
         span = pl.ds(m * 256, 256)
         dnormed[span, :] = lax.dot_general(
             dpreact[span, :], weight_in[...], across_cols, preferred_element_type=F32
         )
 
-    reducer.scatter(2)
+    reducer.scatter(3)
 
     def norm_back(i, carry):
         span = rows(i * STEP, STEP)
@@ -633,7 +634,6 @@
 
     lax.fori_loop(0, CELLS // STEP, norm_back, 0, unroll=2)
     halo_back = Halo(here, gband, edges2, top2, got2, got_top2, hs2, hr2)
-    reducer.scatter(3)
     halo_back.gather_edges(owned)
     halo_back.start()
 

time: 61.3 us -> 61.1 us (level)
  no operation moved by 1% of the time
where the time goes in v6:
time: 61.1 us; the launch traced here: 61 us
  Pallas kernels  59.7 us (98%)
  between operations  1.29 us (2%)
    pallas_call x1, Pallas kernels, block_call(): pl.pallas_call(block_kernel, out_shape=(jax.ShapeDtypeStruct((CELLS, C),...  56.9 us
    pallas_call x1, Pallas kernels, results_call(): pl.pallas_call(functools.partial(results_kernel, norm), out_shape=tuple((...  2.8 us

profile of v6, /device:TPU:1, one launch (start us, length us, event | category | flops | bytes accessed | tf_op | source)
XLA Modules:
  0.0 61.0 jit_solution(12297137202569562371)
XLA Ops:
  1.3 56.9 %shard_map.144 = (bf16[768,256]{1,0:T(8,128)(2,1)}, bf16[768,256]{1,0:T(8,128)(2,1)}, bf16[2,2048,128]{2,1,0:T(8,128)(2,1)}, f32[2,64,128]{2,1,0:T(8,128)}) custom-call(s32[1]{0:T(128)S(6)} %copy.16.owned_ref, s32[3]{0:T(128)} %ocean_ref.1, bf16[768,256]{1,0:T(8,128)(2,1)} %bitcast.8, bf16[768,256]{1,0:T(8,128)(2,1)} %bitcast.9, ...), custom_call_target="tpu_custom_call" | custom-call | tf_op jit(solution)/shard_map/pallas_call | solution.py:795
  58.2 2.8 %shard_map.145 = (bf16[768,256]{1,0:T(8,128)(2,1)}, bf16[768,256]{1,0:T(8,128)(2,1)}, f32[7,7,256]{2,1,0:T(8,128)}, f32[1,256]{1,0:T(1,128)}, f32[256,1024]{1,0:...) custom-call(bf16[768,256]{1,0:T(8,128)(2,1)} %get-tuple-element.18.state_hbm, ...), custom_call_target="tpu_custom_call" | custom-call | tf_op jit(solution)/shard_map/pallas_call | solution.py:877
